TPU v7x, 256 devices: a whole 4x4x8 slice. The times are simulated.
256 devices in a mesh: wide: 64 (over x, z_lo, y, core), narrow: 4 (over z_hi).
Axes of the slice: x: 4, y: 4, z: 8 (z_hi: 4, z_lo: 2; z = z_hi * 2 + z_lo), core: 2. Of those that a mesh axis runs over, the one named last changes fastest.
Arguments:
- source_features: bfloat16 [64, 128, 1024], P('wide'), may hold values from -6 to 6
- target_features: bfloat16 [32, 128, 1024], P('narrow', 'wide'), may hold values from -6 to 6
- target_in_taps: float32 [16, 9], replicated, may hold values from -2 to 2
- target_in_bias: float32 [16], replicated, may hold values from -3 to 3
- target_out_taps: float32 [16, 9], replicated, may hold values from -1 to 1
- source_in_taps: float32 [16, 9], replicated, may hold values from -2 to 2
- source_in_bias: float32 [16], replicated, may hold values from -3 to 3
- source_out_taps: float32 [16, 9], replicated, may hold values from -1 to 1
Outputs:
- consensus: bfloat16 [32, 128, 64, 128], P('narrow', 'wide')
All inputs are finite; a program needn't handle non-finite values.
Results may differ from a plain program's by a relative error of at most 0.0072.
Values may be sent and summed in bfloat16 or wider, within the bound.
A program may use at most 192 MiB of HBM per device.

v0:
```python
import jax
import jax.numpy as jnp
from jax import lax
from jax.sharding import PartitionSpec as P


def padded_2(block, sides, width):
    for axis, dim in sides:
        count = lax.axis_size(axis)
        forward = [(i, i + 1) for i in range(count - 1)]
        backward = [(target, source) for source, target in forward]
        low = lax.ppermute(
            lax.slice_in_dim(block, block.shape[dim] - width, None, axis=dim), axis, forward
        )
        high = lax.ppermute(lax.slice_in_dim(block, 0, width, axis=dim), axis, backward)
        block = jnp.concatenate([low, block, high], axis=dim)
    return block


def conv_valid(field, weights, first_axis, second_axis):
    size_one = field.shape[first_axis] - 2
    size_two = field.shape[second_axis] - 2
    total = None
    for a in range(3):
        rows = lax.slice_in_dim(field, a, a + size_one, axis=first_axis)
        for b in range(3):
            term = weights[3 * a + b] * lax.slice_in_dim(rows, b, b + size_two, axis=second_axis)
            total = term if total is None else total + term
    return total


def pad_axis(field, axis):
    widths = [(0, 0)] * field.ndim
    widths[axis] = (1, 1)
    return jnp.pad(field, widths)


def consensus_section(field, in_taps, in_bias, out_taps, first_axis, second_axis):
    padded = pad_axis(pad_axis(field.astype(jnp.float32), first_axis), second_axis)
    total = None
    for h in range(in_taps.shape[0]):
        hidden = jnp.maximum(
            conv_valid(padded, in_taps[h], first_axis, second_axis) + in_bias[h], 0.0
        )
        hidden = pad_axis(pad_axis(hidden, first_axis), second_axis)
        term = conv_valid(hidden, out_taps[h], first_axis, second_axis)
        total = term if total is None else total + term
    return jnp.maximum(total, 0.0)


def on_device(
    source_features,
    target_features,
    target_in_taps,
    target_in_bias,
    target_out_taps,
    source_in_taps,
    source_in_bias,
    source_out_taps,
):
    src_rows, src_cols, channels = source_features.shape
    tgt_rows = target_features.shape[0]
    scale = channels ** (-0.5)
    flat_source = source_features.reshape(src_rows * src_cols, channels)
    piece = lax.all_gather(target_features, "wide", axis=1, tiled=True)
    count = piece.shape[1]
    product = (
        jnp.dot(
            piece.reshape(tgt_rows * count, channels),
            flat_source.T,
            preferred_element_type=jnp.float32,
        )
        * scale
    )
    correlation = product.astype(jnp.bfloat16).reshape(tgt_rows, count, src_rows, src_cols)
    hidden_count = target_in_taps.shape[0]
    extended = padded_2(correlation, (("narrow", 0),), 2)
    padded = pad_axis(extended.astype(jnp.float32), 1)
    rows_here = tgt_rows + 2
    row_start = lax.axis_index("narrow") * tgt_rows
    global_rows = row_start - 1 + jnp.arange(rows_here, dtype=jnp.int32)
    all_rows = tgt_rows * lax.axis_size("narrow")
    inside = (
        ((global_rows >= 0) & (global_rows < all_rows))
        .astype(jnp.float32)
        .reshape(rows_here, 1, 1, 1)
    )
    total = None
    for h in range(hidden_count):
        hidden = (
            jnp.maximum(conv_valid(padded, target_in_taps[h], 0, 1) + target_in_bias[h], 0.0)
            * inside
        )
        term = conv_valid(pad_axis(hidden, 1), target_out_taps[h], 0, 1)
        total = term if total is None else total + term
    target_section = jnp.maximum(total, 0.0).astype(jnp.bfloat16)
    sectioned = consensus_section(
        lax.all_to_all(target_section, "wide", split_axis=1, concat_axis=2, tiled=True),
        source_in_taps,
        source_in_bias,
        source_out_taps,
        2,
        3,
    )
    return sectioned.astype(jnp.bfloat16)


def solution(mesh):
    placed = (P("wide", None, None), P("narrow", "wide", None), P(), P(), P(), P(), P(), P())
    return jax.shard_map(
        on_device,
        mesh=mesh,
        in_specs=placed,
        out_specs=P("narrow", "wide", None, None),
        check_vma=False,
    )
```

profile of v0, /device:TPU:1, one launch (start us, length us, event | category | flops | bytes accessed | tf_op | source)
XLA Modules:
  0.0 642.1 jit_solution(14112754118471764952)
XLA Ops:
  69.0 50.2 %all-gather.2.cloned.1.call-done = bf16[8,128,1024]{2,0,1:T(8,128)(2,1)} async-done(((bf16[8,2,1024]{2,0,1:T(8,128)(2,1)}), bf16[8,128,1024]{2,0,1:T(8,128)(2,1)}) %all-gather.2.cloned.1.call-update) | async-done | bytes 2097168 | tf_op jit(solution)/shard_map/all_gather | solution.py:65
  131.0 7.3 %maximum_multiply_fusion.15 = f32[10,128,1,128]{3,0,2,1:T(8,128)S(1)} fusion(f32[10]{0:T(128)S(1)} %and_convert_fusion, f32[]{:T(128)} %bitcast.17, f32[]{:T(128)} %bitcast.16, f32[]{:T(128)} %bitcast.15, f32[]{:T(128)} %bitcast.14, f32[]{:T(128)} %bitcast.13, f32[]{:T(128)} %bitcast.12, f32[]{:T(128)} %bitcast.11, f32[]{:T(128)} %bitcast.10, f32[]{:T(128)} %bitcast.9, ...), kind=kLoop, calls=%fused_computation.119 | loop fusion | flops 3276800 | bytes 4850216 | tf_op jit(solution)/shard_map/mul | solution.py:91
  141.3 7.4 %maximum_multiply_fusion = f32[10,128,1,128]{3,0,2,1:T(8,128)S(1)} fusion(f32[]{:T(128)} %bitcast.302, f32[]{:T(128)} %bitcast.301, f32[]{:T(128)} %bitcast.300, f32[]{:T(128)} %bitcast.299, f32[]{:T(128)} %bitcast.298, f32[]{:T(128)} %bitcast.297, f32[]{:T(128)} %bitcast.296, f32[]{:T(128)} %bitcast.295, f32[]{:T(128)} %bitcast.294, f32[]{:T(128)} %bitcast.293, ...), kind=kLoop, calls=%fused_computation.104 | loop fusion | flops 3276800 | bytes 4850216 | tf_op jit(solution)/shard_map/mul | solution.py:91
  148.6 7.3 %maximum_multiply_fusion.1 = f32[10,128,1,128]{3,0,2,1:T(8,128)S(1)} fusion(f32[]{:T(128)} %bitcast.283, f32[]{:T(128)} %bitcast.282, f32[]{:T(128)} %bitcast.281, f32[]{:T(128)} %bitcast.280, f32[]{:T(128)} %bitcast.279, f32[]{:T(128)} %bitcast.278, f32[]{:T(128)} %bitcast.277, f32[]{:T(128)} %bitcast.276, f32[]{:T(128)} %bitcast.275, f32[]{:T(128)} %bitcast.274, ...), kind=kLoop, calls=%fused_computation.105 | loop fusion | flops 3276800 | bytes 4850216 | tf_op jit(solution)/shard_map/mul | solution.py:91
  163.1 8.2 %maximum_multiply_fusion.3 = f32[10,128,1,128]{3,0,2,1:T(8,128)} fusion(f32[]{:T(128)} %bitcast.245, f32[]{:T(128)} %bitcast.244, f32[]{:T(128)} %bitcast.243, f32[]{:T(128)} %bitcast.242, f32[]{:T(128)} %bitcast.241, f32[]{:T(128)} %bitcast.240, f32[]{:T(128)} %bitcast.239, f32[]{:T(128)} %bitcast.238, f32[]{:T(128)} %bitcast.237, f32[]{:T(128)} %bitcast.236, ...), kind=kLoop, calls=%fused_computation.107 | loop fusion | flops 3276800 | bytes 4850216 | tf_op jit(solution)/shard_map/mul | solution.py:91
  171.3 8.1 %maximum_multiply_fusion.4 = f32[10,128,1,128]{3,0,2,1:T(8,128)} fusion(f32[]{:T(128)} %bitcast.226, f32[]{:T(128)} %bitcast.225, f32[]{:T(128)} %bitcast.224, f32[]{:T(128)} %bitcast.223, f32[]{:T(128)} %bitcast.222, f32[]{:T(128)} %bitcast.221, f32[]{:T(128)} %bitcast.220, f32[]{:T(128)} %bitcast.219, f32[]{:T(128)} %bitcast.218, f32[]{:T(128)} %bitcast.217, ...), kind=kLoop, calls=%fused_computation.108 | loop fusion | flops 3276800 | bytes 4850216 | tf_op jit(solution)/shard_map/mul | solution.py:91
  179.4 8.1 %maximum_multiply_fusion.5 = f32[10,128,1,128]{3,0,2,1:T(8,128)} fusion(f32[]{:T(128)} %bitcast.207, f32[]{:T(128)} %bitcast.206, f32[]{:T(128)} %bitcast.205, f32[]{:T(128)} %bitcast.204, f32[]{:T(128)} %bitcast.203, f32[]{:T(128)} %bitcast.202, f32[]{:T(128)} %bitcast.201, f32[]{:T(128)} %bitcast.200, f32[]{:T(128)} %bitcast.199, f32[]{:T(128)} %bitcast.198, ...), kind=kLoop, calls=%fused_computation.109 | loop fusion | flops 3276800 | bytes 4850216 | tf_op jit(solution)/shard_map/mul | solution.py:91
  187.6 8.0 %maximum_multiply_fusion.6 = f32[10,128,1,128]{3,0,2,1:T(8,128)} fusion(f32[]{:T(128)} %bitcast.188, f32[]{:T(128)} %bitcast.187, f32[]{:T(128)} %bitcast.186, f32[]{:T(128)} %bitcast.185, f32[]{:T(128)} %bitcast.184, f32[]{:T(128)} %bitcast.183, f32[]{:T(128)} %bitcast.182, f32[]{:T(128)} %bitcast.181, f32[]{:T(128)} %bitcast.180, f32[]{:T(128)} %bitcast.179, ...), kind=kLoop, calls=%fused_computation.110 | loop fusion | flops 3276800 | bytes 4850216 | tf_op jit(solution)/shard_map/mul | solution.py:91
  195.6 7.9 %maximum_multiply_fusion.7 = f32[10,128,1,128]{3,0,2,1:T(8,128)} fusion(f32[]{:T(128)} %bitcast.169, f32[]{:T(128)} %bitcast.168, f32[]{:T(128)} %bitcast.167, f32[]{:T(128)} %bitcast.166, f32[]{:T(128)} %bitcast.165, f32[]{:T(128)} %bitcast.164, f32[]{:T(128)} %bitcast.163, f32[]{:T(128)} %bitcast.162, f32[]{:T(128)} %bitcast.161, f32[]{:T(128)} %bitcast.160, ...), kind=kLoop, calls=%fused_computation.111 | loop fusion | flops 3276800 | bytes 4850216 | tf_op jit(solution)/shard_map/mul | solution.py:91
  203.4 8.2 %maximum_multiply_fusion.8 = f32[10,128,1,128]{3,0,2,1:T(8,128)} fusion(f32[]{:T(128)} %bitcast.150, f32[]{:T(128)} %bitcast.149, f32[]{:T(128)} %bitcast.148, f32[]{:T(128)} %bitcast.147, f32[]{:T(128)} %bitcast.146, f32[]{:T(128)} %bitcast.145, f32[]{:T(128)} %bitcast.144, f32[]{:T(128)} %bitcast.143, f32[]{:T(128)} %bitcast.142, f32[]{:T(128)} %bitcast.141, ...), kind=kLoop, calls=%fused_computation.112 | loop fusion | flops 3276800 | bytes 4850216 | tf_op jit(solution)/shard_map/mul | solution.py:91
  211.6 8.3 %maximum_multiply_fusion.9 = f32[10,128,1,128]{3,0,2,1:T(8,128)} fusion(f32[]{:T(128)} %bitcast.131, f32[]{:T(128)} %bitcast.130, f32[]{:T(128)} %bitcast.129, f32[]{:T(128)} %bitcast.128, f32[]{:T(128)} %bitcast.127, f32[]{:T(128)} %bitcast.126, f32[]{:T(128)} %bitcast.125, f32[]{:T(128)} %bitcast.124, f32[]{:T(128)} %bitcast.123, f32[]{:T(128)} %bitcast.122, ...), kind=kLoop, calls=%fused_computation.113 | loop fusion | flops 3276800 | bytes 4850216 | tf_op jit(solution)/shard_map/mul | solution.py:91
  220.0 8.2 %maximum_multiply_fusion.10 = f32[10,128,1,128]{3,0,2,1:T(8,128)} fusion(f32[]{:T(128)} %bitcast.112, f32[]{:T(128)} %bitcast.111, f32[]{:T(128)} %bitcast.110, f32[]{:T(128)} %bitcast.109, f32[]{:T(128)} %bitcast.108, f32[]{:T(128)} %bitcast.107, f32[]{:T(128)} %bitcast.106, f32[]{:T(128)} %bitcast.105, f32[]{:T(128)} %bitcast.104, f32[]{:T(128)} %bitcast.103, ...), kind=kLoop, calls=%fused_computation.114 | loop fusion | flops 3276800 | bytes 4850216 | tf_op jit(solution)/shard_map/mul | solution.py:91
  228.2 8.4 %maximum_multiply_fusion.11 = f32[10,128,1,128]{3,0,2,1:T(8,128)} fusion(f32[]{:T(128)} %bitcast.93, f32[]{:T(128)} %bitcast.92, f32[]{:T(128)} %bitcast.91, f32[]{:T(128)} %bitcast.90, f32[]{:T(128)} %bitcast.89, f32[]{:T(128)} %bitcast.88, f32[]{:T(128)} %bitcast.87, f32[]{:T(128)} %bitcast.86, f32[]{:T(128)} %bitcast.85, f32[]{:T(128)} %bitcast.84, ...), kind=kLoop, calls=%fused_computation.115 | loop fusion | flops 3276800 | bytes 4850216 | tf_op jit(solution)/shard_map/mul | solution.py:91
  236.5 8.1 %maximum_multiply_fusion.12 = f32[10,128,1,128]{3,0,2,1:T(8,128)} fusion(f32[]{:T(128)} %bitcast.74, f32[]{:T(128)} %bitcast.73, f32[]{:T(128)} %bitcast.72, f32[]{:T(128)} %bitcast.71, f32[]{:T(128)} %bitcast.70, f32[]{:T(128)} %bitcast.69, f32[]{:T(128)} %bitcast.68, f32[]{:T(128)} %bitcast.67, f32[]{:T(128)} %bitcast.66, f32[]{:T(128)} %bitcast.65, ...), kind=kLoop, calls=%fused_computation.116 | loop fusion | flops 3276800 | bytes 4850216 | tf_op jit(solution)/shard_map/mul | solution.py:91
  244.6 8.4 %maximum_multiply_fusion.13 = f32[10,128,1,128]{3,0,2,1:T(8,128)} fusion(f32[]{:T(128)} %bitcast.55, f32[]{:T(128)} %bitcast.54, f32[]{:T(128)} %bitcast.53, f32[]{:T(128)} %bitcast.52, f32[]{:T(128)} %bitcast.51, f32[]{:T(128)} %bitcast.50, f32[]{:T(128)} %bitcast.49, f32[]{:T(128)} %bitcast.48, f32[]{:T(128)} %bitcast.47, f32[]{:T(128)} %bitcast.46, ...), kind=kLoop, calls=%fused_computation.117 | loop fusion | flops 3276800 | bytes 4850216 | tf_op jit(solution)/shard_map/mul | solution.py:91
  253.0 8.4 %maximum_multiply_fusion.14 = f32[10,128,1,128]{3,0,2,1:T(8,128)} fusion(f32[]{:T(128)} %bitcast.36, f32[]{:T(128)} %bitcast.35, f32[]{:T(128)} %bitcast.34, f32[]{:T(128)} %bitcast.33, f32[]{:T(128)} %bitcast.32, f32[]{:T(128)} %bitcast.31, f32[]{:T(128)} %bitcast.30, f32[]{:T(128)} %bitcast.29, f32[]{:T(128)} %bitcast.28, f32[]{:T(128)} %bitcast.27, ...), kind=kLoop, calls=%fused_computation.118 | loop fusion | flops 3276800 | bytes 4850216 | tf_op jit(solution)/shard_map/mul | solution.py:91
  261.4 133.5 %fusion.610 = bf16[8,128,1,128]{3,0,2,1:T(8,128)(2,1)} fusion(f32[10,128,1,128]{3,0,2,1:T(8,128)S(1)} %maximum_multiply_fusion, f32[]{:T(128)} %bitcast.310, f32[]{:T(128)} %bitcast.309, f32[]{:T(128)} %bitcast.308, f32[]{:T(128)} %bitcast.307, f32[]{:T(128)} %bitcast.306, f32[]{:T(128)} %bitcast.305, f32[]{:T(128)} %bitcast.304, f32[]{:T(128)} %bitcast.303, ...), kind=kLoop, calls=%fused_computation.882 | loop fusion | flops 37486592 | bytes 42277376 | tf_op jit(solution)/shard_map/convert_element_type | solution.py:96
  395.0 8.0 %all-to-all-start = ((bf16[8,128,1,128]{3,0,2,1:T(8,128)(2,1)}), bf16[8,128,1,128]{3,0,2,1:T(8,128)(2,1)S(1)}, u32[]{:S(2)}, u32[]{:S(2)}) async-start(bf16[8,128,1,128]{3,0,2,1:T(8,128)(2,1)} %fusion.610), calls=%async_computation | async-start | bytes 524288 | tf_op jit(solution)/shard_map/all_to_all | solution.py:98
  448.3 7.2 %fusion.573 = f32[8,2,64,128]{3,0,1,2:T(8,128)S(1)} fusion(bf16[8,64,2,1,128]{4,0,2,1,3:T(8,128)(2,1)S(1)} %bitcast.887, f32[]{:T(128)} %bitcast.516, f32[]{:T(128)} %bitcast.515, f32[]{:T(128)} %bitcast.514, f32[]{:T(128)} %bitcast.513, f32[]{:T(128)} %bitcast.512, f32[]{:T(128)} %bitcast.511, f32[]{:T(128)} %bitcast.510, f32[]{:T(128)} %bitcast.509, ...), kind=kLoop, calls=%fused_computation.844 | loop fusion | flops 2621440 | bytes 1851432 | tf_op jit(solution)/shard_map/max | solution.py:42
  455.5 7.2 %fusion.566 = f32[8,2,64,128]{3,0,1,2:T(8,128)S(1)} fusion(bf16[8,64,2,1,128]{4,0,2,1,3:T(8,128)(2,1)S(1)} %bitcast.888, f32[]{:T(128)} %bitcast.497, f32[]{:T(128)} %bitcast.496, f32[]{:T(128)} %bitcast.495, f32[]{:T(128)} %bitcast.494, f32[]{:T(128)} %bitcast.493, f32[]{:T(128)} %bitcast.492, f32[]{:T(128)} %bitcast.491, f32[]{:T(128)} %bitcast.490, ...), kind=kLoop, calls=%fused_computation.837 | loop fusion | flops 2621440 | bytes 1851432 | tf_op jit(solution)/shard_map/max | solution.py:42
  498.4 7.2 %fusion.524 = f32[8,2,64,128]{3,0,1,2:T(8,128)S(1)} fusion(bf16[8,64,2,1,128]{4,0,2,1,3:T(8,128)(2,1)S(1)} %bitcast.894, f32[]{:T(128)} %bitcast.383, f32[]{:T(128)} %bitcast.382, f32[]{:T(128)} %bitcast.381, f32[]{:T(128)} %bitcast.380, f32[]{:T(128)} %bitcast.379, f32[]{:T(128)} %bitcast.378, f32[]{:T(128)} %bitcast.377, f32[]{:T(128)} %bitcast.376, ...), kind=kLoop, calls=%fused_computation.795 | loop fusion | flops 2621440 | bytes 1851432 | tf_op jit(solution)/shard_map/max | solution.py:42
  512.8 7.3 %fusion.510 = f32[8,2,64,128]{3,0,1,2:T(8,128)S(1)} fusion(bf16[8,64,2,1,128]{4,0,2,1,3:T(8,128)(2,1)S(1)} %bitcast.896, f32[]{:T(128)} %bitcast.345, f32[]{:T(128)} %bitcast.344, f32[]{:T(128)} %bitcast.343, f32[]{:T(128)} %bitcast.342, f32[]{:T(128)} %bitcast.341, f32[]{:T(128)} %bitcast.339, f32[]{:T(128)} %bitcast.338, f32[]{:T(128)} %bitcast.337, ...), kind=kLoop, calls=%fused_computation.781 | loop fusion | flops 2621440 | bytes 1851432 | tf_op jit(solution)/shard_map/max | solution.py:42
  520.2 7.7 %broadcast_multiply_fusion = (f32[8,2,64,128]{3,0,1,2:T(8,128)S(1)}, f32[8,2,64,128]{3,0,1,2:T(8,128)S(1)}) fusion(f32[]{:T(128)} %bitcast.329, f32[]{:T(128)} %bitcast.325, f32[]{:T(128)} %bitcast.324, f32[]{:T(128)} %bitcast.323, f32[]{:T(128)} %bitcast.322, f32[]{:T(128)} %bitcast.321, bf16[8,64,2,1,128]{4,0,2,1,3:T(8,128)(2,1)S(1)} %bitcast.897, ...), kind=kLoop, calls=%fused_computation.884 | loop fusion | flops 2752512 | bytes 2375724 | tf_op jit(solution)/shard_map/mul | solution.py:27
  527.9 106.1 %fusion.609 = bf16[8,2,64,128]{3,0,1,2:T(8,128)(2,1)S(1)} fusion(f32[8,2,66,128]{3,0,1,2:T(8,128)S(1)} %pad.206, f32[8,2,64,128]{3,0,1,2:T(8,128)S(1)} %fusion.608, f32[]{:T(128)} %bitcast.619, f32[]{:T(128)} %bitcast.618, f32[]{:T(128)} %bitcast.617, f32[]{:T(128)} %bitcast.616, f32[]{:T(128)} %bitcast.615, f32[]{:T(128)} %bitcast.614, f32[]{:T(128)} %bitcast.613, ...), kind=kLoop, calls=%fused_computation.881 | loop fusion | flops 37748736 | bytes 34079292 | tf_op jit(solution)/shard_map/convert_element_type | solution.py:105
  (90 shorter events, 173.0 us)
Async XLA Ops:
  6.5 115.4 %copy-start = (bf16[1,128,1024]{2,1,0:T(8,128)(2,1)S(1)}, bf16[1,128,1024]{2,1,0:T(8,128)(2,1)}, u32[]{:S(2)}) copy-start(bf16[1,128,1024]{2,1,0:T(8,128)(2,1)} %param.8) | copy-start | bytes 786436
  6.5 112.7 %all-gather.2.cloned.1.call-start = ((), (), s32[]{:S(2)}) async-start(), calls=%async_computation.1 | async-start | bytes 2129920 | tf_op jit(solution)/shard_map/all_gather | solution.py:65
  122.8 7.9 %collective-permute-start.1 = (bf16[2,128,1,128]{3,0,2,1:T(2,128)(2,1)S(1)}, bf16[2,128,1,128]{3,0,2,1:T(2,128)(2,1)S(1)}, u32[]{:S(2)}, u32[]{:S(2)}) collective-permute-start(bf16[2,128,1,128]{3,0,2,1:T(2,128)(2,1)S(1)} %copy.22), channel_id=1, source_target_pairs={{1,0},{2,1},{3,2},{5,4},{6,5},{7,6},{9,8},{10,9},{11,10},{13,12},{... | collective-permute-start | bytes 196616 | tf_op jit(solution)/shard_map/ppermute | solution.py:15
  124.1 6.5 %collective-permute-start = (bf16[2,128,1,128]{3,0,2,1:T(2,128)(2,1)S(1)}, bf16[2,128,1,128]{3,0,2,1:T(2,128)(2,1)S(1)}, u32[]{:S(2)}, u32[]{:S(2)}) collective-permute-start(bf16[2,128,1,128]{3,0,2,1:T(2,128)(2,1)S(1)} %copy.21), channel_id=1, source_target_pairs={{0,1},{1,2},{2,3},{4,5},{5,6},{6,7},{8,9},{9,10},{10,11},{12,13},{... | collective-permute-start | bytes 196616 | tf_op jit(solution)/shard_map/ppermute | solution.py:12
  138.2 3.0 copy-start.1
  261.4 141.6 %copy-start.2 = (f32[16,9]{1,0:T(8,128)S(1)}, f32[16,9]{1,0:T(8,128)}, u32[]{:S(2)}) copy-start(f32[16,9]{1,0:T(8,128)} %param.15) | copy-start | bytes 1732
  261.4 142.3 %copy-start.3 = (f32[16,9]{1,0:T(8,128)S(1)}, f32[16,9]{1,0:T(8,128)}, u32[]{:S(2)}) copy-start(f32[16,9]{1,0:T(8,128)} %param.13) | copy-start | bytes 1732
  395.0 17.6 %all-to-all-start = ((bf16[8,128,1,128]{3,0,2,1:T(8,128)(2,1)}), bf16[8,128,1,128]{3,0,2,1:T(8,128)(2,1)S(1)}, u32[]{:S(2)}, u32[]{:S(2)}) async-start(bf16[8,128,1,128]{3,0,2,1:T(8,128)(2,1)} %fusion.610), calls=%async_computation | async-start | bytes 524288 | tf_op jit(solution)/shard_map/all_to_all | solution.py:98
Sparse Core Ops, SparseCore 0:
  9.2 109.9 all-gather.1
where the time goes:
time: 654 us; the launch traced here: 642 us
  other arithmetic  485 us (74%)
  local copies, waits for them, and re-layouts  70.3 us (11%)
  waiting for transfers between devices  57.2 us (9%)
  starting transfers between devices  14.7 us (2%)
  between operations  14.4 us (2%)
    convert_element_type x1, other arithmetic, on_device(): target_section = jnp.maximum(total, 0.0).astype(jnp.bfloat16)  134 us
    mul x16, other arithmetic, on_device(): jnp.maximum(conv_valid(padded, target_in_taps[h], 0, 1) + target_in_bias[...  127 us
    max x15, other arithmetic, consensus_section(): jnp.maximum(conv_valid(padded, in_taps[h], first_axis, second_axis) + in_...  107 us
    convert_element_type x1, other arithmetic, on_device(): return sectioned.astype(jnp.bfloat16)  106 us
    slice x32, local copies, waits for them, and re-layouts, conv_valid(): weights[3 * a + b]  60.5 us
    all_gather x1, waiting for transfers between devices, on_device(): piece = lax.all_gather(target_features, 'wide', axis=1, tiled=True)  50.2 us
  transfers between devices with their start and end apart: 4, of which 3 were waited for; matrix products, arithmetic and copies ran while one was open for 10% of the time, Pallas kernels for 0%

commit v1 on v0

v1 whole, which is shorter than its diff:
```python
import functools

import jax
import jax.numpy as jnp
from jax import lax
from jax.experimental import pallas as pl
from jax.experimental.pallas import tpu as pltpu
from jax.sharding import PartitionSpec as P

F32 = jnp.float32
BF16 = jnp.bfloat16
OFF = -1e38


def split(value):
    high = value.astype(BF16)
    return high, (value - high.astype(F32)).astype(BF16)


def build_target_weights(in_taps_ref, out_taps_ref, w1_hi, w1_lo, w2):
    def chunk(c, carry):
        shape = (256, 256)
        row = lax.broadcasted_iota(jnp.int32, shape, 0)
        cell = (lax.broadcasted_iota(jnp.int32, shape, 1) + c * 256) >> 4
        l_hid = (cell * 205) >> 11
        k_hid = cell - l_hid * 10
        code = ((row >> 4) - l_hid) * 16 + (((row & 15) - k_hid + 2) & 15)
        lanes = pl.ds(pl.multiple_of(c * 256, 256), 256)
        value = jnp.zeros(shape, F32)
        for a in range(3):
            for b in range(3):
                n = 3 * a + b
                taps = in_taps_ref[n : n + 1, :]
                value = jnp.where(code == b * 16 + a, taps, value)
        high, low = split(value)
        w1_hi[:, lanes] = high
        w1_lo[:, lanes] = low

        shape = (16, 1, 128)
        cell = lax.broadcasted_iota(jnp.int32, shape, 0) + c * 16
        lane = lax.broadcasted_iota(jnp.int32, shape, 2)
        l_hid = (cell * 205) >> 11
        k_hid = cell - l_hid * 10
        code = (l_hid - (lane >> 3)) * 16 + ((k_hid - (lane & 7)) & 15)
        code = jnp.broadcast_to(code, (16, 16, 128))
        value = jnp.zeros((16, 16, 128), F32)
        for a in range(3):
            for b in range(3):
                taps = out_taps_ref[3 * a + b]
                value = jnp.where(code == b * 16 + a, taps[None], value)
        high, low = split(value.reshape(256, 128))
        rows = pl.ds(pl.multiple_of(c * 256, 256), 256)
        w2[rows, 0:128] = high
        w2[rows, 128:256] = low
        return carry

    lax.fori_loop(0, 9, chunk, 0)


def target_section(block, x_t, bias_ref, w1_hi, w1_lo, w2, x, bias, acc, out):
    for p in range(11):
        part = x_t[p * 192 : p * 192 + 256, :].astype(F32)
        x[p * 128 : (p + 1) * 128, :] = part.T.astype(BF16)
    shape = (11, 2304)
    patch = lax.broadcasted_iota(jnp.int32, shape, 0)
    cell = lax.broadcasted_iota(jnp.int32, shape, 1) >> 4
    l_hid = (cell * 205) >> 11
    k_at = cell - l_hid * 10 - 1 + block * 8
    l_at = patch * 12 - 1 + l_hid
    valid = (l_at >= 0) & (l_at < 128) & (k_at >= 0) & (k_at < 32) & (cell < 140)
    bias[...] = jnp.where(valid, bias_ref[...], OFF)

    acc[...] = jnp.zeros_like(acc)
    for c in range(9):
        lanes = slice(c * 256, (c + 1) * 256)
        hidden = jnp.dot(x[...], w1_hi[:, lanes], preferred_element_type=F32)
        hidden += jnp.dot(x[...], w1_lo[:, lanes], preferred_element_type=F32)
        hidden = hidden.reshape(11, 128, 256) + bias[:, lanes][:, None, :]
        hidden = jnp.maximum(hidden, 0.0).reshape(1408, 256)
        high, low = split(hidden)
        acc[...] += jnp.dot(high, w2[lanes, :], preferred_element_type=F32)
        acc[:, 0:128] += jnp.dot(low, w2[lanes, 0:128], preferred_element_type=F32)
    for p in range(11):
        rows = slice(p * 128, (p + 1) * 128)
        total = jnp.maximum(acc[rows, 0:128] + acc[rows, 128:256], 0.0).T
        count = 96 if p < 10 else 64
        out[p * 96 : p * 96 + count, :] = total[:count].astype(BF16)


def target_kernel(x_t, in_taps, in_bias, out_taps, out, w1_hi, w1_lo, w2, x, bias, acc):
    build_target_weights(in_taps, out_taps, w1_hi, w1_lo, w2)
    block = lax.axis_index("narrow")
    target_section(block, x_t, in_bias, w1_hi, w1_lo, w2, x, bias, acc, out)


def source_kernel(r_ref, in_taps, in_bias, out_taps, out_ref, w1, w2, x, acc, turned):
    def band(h, carry):
        shape = (128, 128)
        apart = lax.broadcasted_iota(jnp.int32, shape, 0) - lax.broadcasted_iota(
            jnp.int32, shape, 1
        )
        c, at = h // 2, pl.multiple_of((h % 2) * 128, 128)
        for a in range(3):
            for taps, w, first in ((in_taps, w1, True), (out_taps, w2, False)):
                value = jnp.zeros(shape, F32)
                for b in range(3):
                    value = jnp.where(apart == b - 1, taps[h, 3 * a + b], value)
                for n, part in enumerate(split(value)):
                    other = slice((3 * n + a) * 128, (3 * n + a + 1) * 128)
                    if first:
                        w[c, other, pl.ds(at, 128)] = part
                    else:
                        w[c, pl.ds(at, 128), other] = part
        return carry

    lax.fori_loop(0, 16, band, 0)

    zero = jnp.zeros((16, 128), BF16)
    for n in range(2):
        at = n * 384
        x[0:16, at : at + 128] = zero
        x[16:1024, at : at + 128] = r_ref[0:1008, :]
        x[:, at + 128 : at + 256] = r_ref[...]
        x[0:1008, at + 256 : at + 384] = r_ref[16:1024, :]
        x[1008:1024, at + 256 : at + 384] = zero

    acc[...] = jnp.zeros_like(acc)
    for c in range(8):
        hidden = jnp.dot(x[...], w1[c], preferred_element_type=F32)
        hidden = jnp.maximum(hidden + in_bias[:, c * 256 : (c + 1) * 256], 0.0)
        high, low = split(hidden)
        both = jnp.dot(high, w2[c], preferred_element_type=F32)
        rest = jnp.dot(low, w2[c, :, 0:384], preferred_element_type=F32)
        acc[...] += both[:, 0:384] + both[:, 384:768] + rest
    for i in range(64):
        rows = slice(i * 16, (i + 1) * 16)
        total = acc[rows, 128:256]
        if i > 0:
            total += acc[i * 16 - 16 : i * 16, 0:128]
        if i < 63:
            total += acc[i * 16 + 16 : i * 16 + 32, 256:384]
        turned[pl.ds(i, 16, stride=64), :] = jnp.maximum(total, 0.0)
    for k in range(8):
        for l in range(2):
            n = l * 8 + k
            out_ref[k, l] = turned[n * 64 : (n + 1) * 64, :].astype(BF16)


VMEM = pl.BlockSpec(memory_space=pltpu.VMEM)
SMEM = pl.BlockSpec(memory_space=pltpu.SMEM)


def on_device(
    source_features,
    target_features,
    target_in_taps,
    target_in_bias,
    target_out_taps,
    source_in_taps,
    source_in_bias,
    source_out_taps,
):
    scale = source_features.shape[-1] ** (-0.5)
    local = jnp.swapaxes(target_features, 0, 1).reshape(16, 1024)
    flat = lax.all_gather(local, "wide", axis=0, tiled=True)
    product = jnp.dot(flat, source_features[0].T, preferred_element_type=F32) * scale
    cells = product.astype(BF16).reshape(128, 8, 128)
    up = [(i, i + 1) for i in range(3)]
    down = [(i + 1, i) for i in range(3)]
    below = lax.ppermute(cells[:, 6:8], "narrow", up)
    above = lax.ppermute(cells[:, 0:2], "narrow", down)
    gap = jnp.zeros((128, 4, 128), BF16)
    x_t = jnp.concatenate([cells, above, gap, below], axis=1)
    x_t = jnp.pad(x_t, ((2, 6), (0, 0), (0, 0))).reshape(136 * 16, 128)
    section = pl.pallas_call(
        target_kernel,
        out_shape=jax.ShapeDtypeStruct((1024, 128), BF16),
        in_specs=[VMEM] * 4,
        out_specs=VMEM,
        scratch_shapes=[
            pltpu.VMEM((256, 2304), BF16),
            pltpu.VMEM((256, 2304), BF16),
            pltpu.VMEM((2304, 256), BF16),
            pltpu.VMEM((1408, 256), BF16),
            pltpu.VMEM((11, 2304), F32),
            pltpu.VMEM((1408, 256), F32),
        ],
        compiler_params=pltpu.CompilerParams(vmem_limit_bytes=48 * 2**20),
    )(
        x_t,
        jnp.tile(target_in_taps.T, (1, 16)),
        jnp.tile(target_in_bias, 144)[None],
        jnp.broadcast_to(target_out_taps.T[:, :, None], (9, 16, 128)),
    )
    received = lax.all_to_all(
        section.reshape(64, 16, 128), "wide", split_axis=0, concat_axis=0, tiled=True
    )
    return pl.pallas_call(
        source_kernel,
        out_shape=jax.ShapeDtypeStruct((8, 2, 64, 128), BF16),
        in_specs=[VMEM, SMEM, VMEM, SMEM],
        out_specs=VMEM,
        scratch_shapes=[
            pltpu.VMEM((8, 768, 256), BF16),
            pltpu.VMEM((8, 256, 768), BF16),
            pltpu.VMEM((1024, 768), BF16),
            pltpu.VMEM((1024, 384), F32),
            pltpu.VMEM((1024, 128), F32),
        ],
        compiler_params=pltpu.CompilerParams(vmem_limit_bytes=48 * 2**20),
    )(
        received.reshape(1024, 128),
        source_in_taps,
        jnp.repeat(source_in_bias, 128)[None],
        source_out_taps,
    )


def solution(mesh):
    placed = (P("wide", None, None), P("narrow", "wide", None), P(), P(), P(), P(), P(), P())
    return jax.shard_map(
        on_device,
        mesh=mesh,
        in_specs=placed,
        out_specs=P("narrow", "wide", None, None),
        check_vma=False,
    )
```

time: 654 us -> 179 us (0.27); the launches traced: 642 us -> 179 us
  other arithmetic: 485 us -> 0.28 us
  local copies, waits for them, and re-layouts: 70.3 us -> 2.23 us
  waiting for transfers between devices: 57.2 us -> 112 us
  Pallas kernels: 0 us -> 24.3 us
  blocking collectives: 0 us -> 17.3 us
  starting transfers between devices: 14.7 us -> 6.21 us
    convert_element_type x5 -> x0, other arithmetic: 240 us -> none  [the longest x1 134 us: on_device(): target_section = jnp.maximum(total, 0.0).astype(jnp.bfloat16)]
    mul x18 -> x0, other arithmetic: 138 us -> none  [the longest x16 127 us: on_device(): jnp.maximum(conv_valid(padded, target_in_taps[h], 0, 1) + target_in_bias[...]
    max x15 -> x0, other arithmetic: 107 us -> none  [consensus_section(): jnp.maximum(conv_valid(padded, in_taps[h], first_axis, second_axis) + in_...]
    slice x37 -> x1, local copies, waits for them, and re-layouts: 64.6 us -> 0.09 us  [on_device(): above = lax.ppermute(cells[:, 0:2], 'narrow', down)]
    all_gather x1, waiting for transfers between devices: 50.2 us -> 111 us  [on_device(): flat = lax.all_gather(local, 'wide', axis=0, tiled=True)]
    pallas_call x0 -> x2, Pallas kernels: none -> 24.3 us  [the longest x1 13.5 us: on_device(): pl.pallas_call(source_kernel, out_shape=jax.ShapeDtypeStruct((8, 2, 64, 1...]
    all_to_all x0 -> x1, blocking collectives: none -> 17.3 us  [on_device(): lax.all_to_all(section.reshape(64, 16, 128), 'wide', split_axis=0, concat...]
    all_to_all x1 -> x0, starting transfers between devices: 8.02 us -> none  [on_device(): lax.all_to_all(target_section, 'wide', split_axis=1, concat_axis=2, tiled...]
  transfers between devices with their start and end apart: 4 -> 3, of which waited for: 3 -> 2; matrix products, arithmetic and copies ran while one was open for 10% -> 0% of each run, Pallas kernels for 0% -> 0%
where the time goes in v1:
time: 179 us
  waiting for transfers between devices  112 us (63%)
  Pallas kernels  24.3 us (14%)
  blocking collectives  17.3 us (10%)
  between operations  13.5 us (8%)
  starting transfers between devices  6.21 us (3%)
  matrix products  2.3 us (1%)
  local copies, waits for them, and re-layouts  2.23 us (1%)
    all_gather x1, waiting for transfers between devices, on_device(): flat = lax.all_gather(local, 'wide', axis=0, tiled=True)  111 us
    all_to_all x1, blocking collectives, on_device(): lax.all_to_all(section.reshape(64, 16, 128), 'wide', split_axis=0, concat...  17.3 us
    pallas_call x1, Pallas kernels, on_device(): pl.pallas_call(source_kernel, out_shape=jax.ShapeDtypeStruct((8, 2, 64, 1...  13.5 us
    pallas_call x1, Pallas kernels, on_device(): pl.pallas_call(target_kernel, out_shape=jax.ShapeDtypeStruct((1024, 128),...  10.7 us
    ppermute x1, starting transfers between devices, on_device(): below = lax.ppermute(cells[:, 6:8], 'narrow', up)  4.89 us
  transfers between devices with their start and end apart: 3, of which 2 were waited for; matrix products, arithmetic and copies ran while one was open for 0% of the time, Pallas kernels for 0%

profile of v1, /device:TPU:1, one launch (start us, length us, event | category | flops | bytes accessed | tf_op | source)
XLA Modules:
  0.0 178.5 jit_solution(3788832515286067336)
XLA Ops:
  6.5 0.0 all-gather.2.cloned.1.call-start
  6.6 1.4 copy.15
  8.0 0.0 all-gather.2.cloned.1.call-update
  8.0 111.2 %all-gather.2.cloned.1.call-done = bf16[1024,1024]{1,0:T(8,128)(2,1)} async-done(((bf16[16,1024]{1,0:T(8,128)(2,1)}), bf16[1024,1024]{1,0:T(8,128)(2,1)}) %all-gather.2.cloned.1.call-update) | async-done | bytes 2097168 | tf_op jit(solution)/shard_map/all_gather | solution.py:165
  119.2 2.3 %fusion.1 = bf16[128,8,128]{2,1,0:T(8,128)(2,1)S(1)} fusion(bf16[1024,1024]{1,0:T(8,128)(2,1)} %all-gather.2.cloned.1.call-done, bf16[1,128,1024]{2,1,0:T(8,128)(2,1)S(1)} %copy-done), kind=kOutput, calls=%fused_computation.2 | convolution fusion | flops 268697600 | bytes 2621440 | tf_op jit(solution)/shard_map/dot_general | solution.py:166
  121.5 0.0 copy-start.6
  121.5 0.0 copy-start.1
  121.6 0.0 copy-start.2
  121.6 0.1 fusion.3
  121.7 1.3 collective-permute-start
  123.0 4.9 %collective-permute-start.1 = (bf16[128,2,128]{2,1,0:T(2,128)(2,1)S(1)}, bf16[128,2,128]{2,1,0:T(2,128)(2,1)S(1)}, u32[]{:S(2)}, u32[]{:S(2)}) collective-permute-start(bf16[128,2,128]{2,1,0:T(2,128)(2,1)S(1)} %get-tuple-element.6), channel_id=1, source_target_pairs={{0,1},{1,2},{2,3},{4,5},{5,6},{6,7},{8,9},{9,10},{10,11},{12,13},{... | collective-permute-start | bytes 196616 | tf_op jit(solution)/shard_map/ppermute | solution.py:170
  127.9 0.1 copy.12
  128.0 0.1 tile.7.in_taps
  128.1 0.1 broadcast_in_dim_tile.3.in_bias
  128.2 0.1 copy.13
  128.3 0.1 pad.7.clone
  128.4 1.2 collective-permute-done
  129.6 0.3 pad_maximum_fusion
  129.9 0.1 pad.4
  130.0 0.1 broadcast_in_dim.13.out_taps
  130.1 10.7 %shard_map.82 = bf16[1024,128]{1,0:T(8,128)(2,1)S(1)} custom-call(bf16[2176,128]{1,0:T(8,128)(2,1)S(1)} %bitcast.17, f32[9,256]{1,0:T(8,128)S(1)} %tile.7.in_taps, f32[1,2304]{1,0:T(1,128)S(1)} %broadcast_in_dim_tile.3.in_bias, f32[9,16,128]{2,1,0:T(8,128)S(1)} %broadcast_in_dim.13.out_taps), custom_call_target="tpu_custom_call" | custom-call | tf_op jit(solution)/shard_map/pallas_call | solution.py:175
  140.8 17.3 %all_to_all.5 = bf16[64,16,128]{2,1,0:T(8,128)(2,1)S(1)} all-to-all(bf16[64,16,128]{2,1,0:T(8,128)(2,1)S(1)} %bitcast.19), channel_id=1, replica_groups=mesh['wide'=64,'narrow'=4] {'wide'}, dimensions={0} | all-to-all | bytes 524288 | tf_op jit(solution)/shard_map/all_to_all | solution.py:195
  158.1 0.1 broadcast_in_dim.14
  158.2 13.5 %shard_map.83 = bf16[8,2,64,128]{3,2,1,0:T(8,128)(2,1)} custom-call(bf16[1024,128]{1,0:T(8,128)(2,1)S(1)} %bitcast.18, f32[16,9]{1,0:T(8,128)S(1)} %copy-done.1, f32[1,2048]{1,0:T(1,128)S(1)} %bitcast.20, f32[16,9]{1,0:T(8,128)S(1)} %copy-done.2), custom_call_target="tpu_custom_call" | custom-call | tf_op jit(solution)/shard_map/pallas_call | solution.py:198
  (15 shorter events, 0.0 us)
Async XLA Ops:
  6.5 112.7 %copy-start = (bf16[1,128,1024]{2,1,0:T(8,128)(2,1)S(1)}, bf16[1,128,1024]{2,1,0:T(8,128)(2,1)}, u32[]{:S(2)}) copy-start(bf16[1,128,1024]{2,1,0:T(8,128)(2,1)} %param.8) | copy-start | bytes 786436
  6.5 121.3 %copy-start.3 = (f32[16,9]{1,0:T(8,128)S(1)}, f32[16,9]{1,0:T(8,128)}, u32[]{:S(2)}) copy-start(f32[16,9]{1,0:T(8,128)} %param.10) | copy-start | bytes 1732
  6.5 121.5 %copy-start.5 = (f32[16]{0:T(128)S(1)}, f32[16]{0:T(128)}, u32[]{:S(2)}) copy-start(f32[16]{0:T(128)} %param.11) | copy-start | bytes 196
  6.5 121.6 %copy-start.4 = (f32[16,9]{1,0:T(8,128)S(1)}, f32[16,9]{1,0:T(8,128)}, u32[]{:S(2)}) copy-start(f32[16,9]{1,0:T(8,128)} %param.12) | copy-start | bytes 1732
  6.5 112.7 %all-gather.2.cloned.1.call-start = ((), (), s32[]{:S(2)}) async-start(), calls=%async_computation.1 | async-start | bytes 2129920 | tf_op jit(solution)/shard_map/all_gather | solution.py:165
  121.5 36.6 %copy-start.6 = (f32[16]{0:T(128)S(1)}, f32[16]{0:T(128)}, u32[]{:S(2)}) copy-start(f32[16]{0:T(128)} %param.14) | copy-start | bytes 196
  121.5 36.6 %copy-start.1 = (f32[16,9]{1,0:T(8,128)S(1)}, f32[16,9]{1,0:T(8,128)}, u32[]{:S(2)}) copy-start(f32[16,9]{1,0:T(8,128)} %in_taps.1) | copy-start | bytes 1732
  121.6 36.6 %copy-start.2 = (f32[16,9]{1,0:T(8,128)S(1)}, f32[16,9]{1,0:T(8,128)}, u32[]{:S(2)}) copy-start(f32[16,9]{1,0:T(8,128)} %out_taps.1) | copy-start | bytes 1732
  121.7 7.9 %collective-permute-start = (bf16[128,2,128]{2,1,0:T(2,128)(2,1)S(1)}, bf16[128,2,128]{2,1,0:T(2,128)(2,1)S(1)}, u32[]{:S(2)}, u32[]{:S(2)}) collective-permute-start(bf16[128,2,128]{2,1,0:T(2,128)(2,1)S(1)} %get-tuple-element.5), channel_id=1, source_target_pairs={{1,0},{2,1},{3,2},{5,4},{6,5},{7,6},{9,8},{10,9},{11,10},{13,12},{... | collective-permute-start | bytes 196616 | tf_op jit(solution)/shard_map/ppermute | solution.py:171
  123.0 6.7 %collective-permute-start.1 = (bf16[128,2,128]{2,1,0:T(2,128)(2,1)S(1)}, bf16[128,2,128]{2,1,0:T(2,128)(2,1)S(1)}, u32[]{:S(2)}, u32[]{:S(2)}) collective-permute-start(bf16[128,2,128]{2,1,0:T(2,128)(2,1)S(1)} %get-tuple-element.6), channel_id=1, source_target_pairs={{0,1},{1,2},{2,3},{4,5},{5,6},{6,7},{8,9},{9,10},{10,11},{12,13},{... | collective-permute-start | bytes 196616 | tf_op jit(solution)/shard_map/ppermute | solution.py:170
Sparse Core Ops, SparseCore 0:
  9.2 109.9 all-gather.1

commit v2 on v1

--- a/solution.py
+++ b/solution.py
@@ -59,7 +59,7 @@
 
 def target_section(block, x_t, bias_ref, w1_hi, w1_lo, w2, x, bias, acc, out):
     for p in range(11):
-        part = x_t[p * 192 : p * 192 + 256, :].astype(F32)
+        part = x_t[p * 192 : p * 192 + 256, :]
         x[p * 128 : (p + 1) * 128, :] = part.T.astype(BF16)
     shape = (11, 2304)
     patch = lax.broadcasted_iota(jnp.int32, shape, 0)
@@ -87,13 +87,7 @@
         out[p * 96 : p * 96 + count, :] = total[:count].astype(BF16)
 
 
-def target_kernel(x_t, in_taps, in_bias, out_taps, out, w1_hi, w1_lo, w2, x, bias, acc):
-    build_target_weights(in_taps, out_taps, w1_hi, w1_lo, w2)
-    block = lax.axis_index("narrow")
-    target_section(block, x_t, in_bias, w1_hi, w1_lo, w2, x, bias, acc, out)
-
-
-def source_kernel(r_ref, in_taps, in_bias, out_taps, out_ref, w1, w2, x, acc, turned):
+def build_source_weights(in_taps, out_taps, w1, w2):
     def band(h, carry):
         shape = (128, 128)
         apart = lax.broadcasted_iota(jnp.int32, shape, 0) - lax.broadcasted_iota(
@@ -115,13 +109,15 @@
 
     lax.fori_loop(0, 16, band, 0)
 
+
+def source_section(r_ref, in_bias, out_ref, w1, w2, x, acc, turned):
     zero = jnp.zeros((16, 128), BF16)
     for n in range(2):
         at = n * 384
         x[0:16, at : at + 128] = zero
-        x[16:1024, at : at + 128] = r_ref[0:1008, :]
-        x[:, at + 128 : at + 256] = r_ref[...]
-        x[0:1008, at + 256 : at + 384] = r_ref[16:1024, :]
+        x[16:1024, at : at + 128] = r_ref[0:63].reshape(1008, 128)
+        x[:, at + 128 : at + 256] = r_ref[...].reshape(1024, 128)
+        x[0:1008, at + 256 : at + 384] = r_ref[1:64].reshape(1008, 128)
         x[1008:1024, at + 256 : at + 384] = zero
 
     acc[...] = jnp.zeros_like(acc)
@@ -146,6 +142,225 @@
             out_ref[k, l] = turned[n * 64 : (n + 1) * 64, :].astype(BF16)
 
 
+MESH = pl.DeviceIdType.MESH
+
+
+def push(src, dst, send_sem, recv_sem, device):
+    return pltpu.make_async_remote_copy(
+        src_ref=src,
+        dst_ref=dst,
+        send_sem=send_sem,
+        recv_sem=recv_sem,
+        device_id=device,
+        device_id_type=MESH,
+    )
+
+
+class Gather:
+    def __init__(self, held, send, recv):
+        me = lax.axis_index("wide")
+        self.narrow = lax.axis_index("narrow")
+        self.held, self.send, self.recv = held, send, recv
+        self.core = me % 2
+        self.at = (me // 16, (me // 2) % 4)
+        self.z = (me // 8) % 2
+        self.count = 0
+        self.copies = []
+
+    def device(self, x=None, y=None, z=None, core=None):
+        x = self.at[0] if x is None else x
+        y = self.at[1] if y is None else y
+        z = self.z if z is None else z
+        core = self.core if core is None else core
+        return (((x * 2 + z) * 4 + y) * 2 + core, self.narrow)
+
+    def partners(self):
+        found = [self.device(z=1 - self.z), self.device(core=1 - self.core)]
+        for axis in "xy":
+            for d in range(1, 4):
+                found.append(self.along(axis, d))
+        return found
+
+    def along(self, axis, d):
+        n = (self.at[0 if axis == "x" else 1] + d) % 4
+        return self.device(**{axis: n})
+
+    def piece(self, half, back, core=None):
+        x, y = ((self.at[n] + 4 - back[n]) % 4 for n in range(2))
+        core = self.core if core is None else core
+        return self.held.at[x, :, y, core, :, half * 512 : half * 512 + 512]
+
+    def start(self, src, arrives, device):
+        n = self.count
+        self.count += 1
+        copy = push(src, src, self.send.at[n], self.recv.at[n], device)
+        copy.start()
+        landed = push(src, arrives, self.send.at[n], self.recv.at[n], device)
+        self.copies.append((copy, landed))
+        return landed
+
+    def first(self):
+        x, y = self.at
+        slot = self.held.at[x, self.z, y, self.core]
+        other = self.held.at[x, 1 - self.z, y, self.core]
+        self.pair = self.start(slot, other, self.device(z=1 - self.z))
+
+    def sibling(self, half, back):
+        self.siblings.append(
+            self.start(
+                self.piece(half, back),
+                self.piece(half, back, 1 - self.core),
+                self.device(core=1 - self.core),
+            )
+        )
+
+    def second(self):
+        self.pair.wait_recv()
+        self.siblings = []
+        self.early, self.late = {}, {}
+        for d in (1, 3, 2):
+            for half in range(2):
+                axis = "xy"[half]
+                back = [0, 0]
+                back[half] = d
+                landed = self.piece(half, back)
+                self.early[half, d] = self.start(
+                    self.piece(half, (0, 0)), landed, self.along(axis, d)
+                )
+        for half in range(2):
+            self.spread(half, 0)
+
+    def spread(self, half, e):
+        back = [0, 0]
+        back[half] = e
+        for d in (1, 3, 2):
+            from_ = list(back)
+            from_[1 - half] = d
+            self.late[half, e, d] = self.start(
+                self.piece(half, back), self.piece(half, from_), self.along("yx"[half], d)
+            )
+        self.sibling(half, back)
+
+    def third(self):
+        for e in (1, 3, 2):
+            for half in range(2):
+                self.early[half, e].wait_recv()
+                self.spread(half, e)
+        for e in (0, 1, 3, 2):
+            for d in (1, 3, 2):
+                for half in range(2):
+                    self.late[half, e, d].wait_recv()
+                    back = [0, 0]
+                    back[half], back[1 - half] = e, d
+                    self.sibling(half, back)
+
+    def finish(self):
+        for landed in self.siblings:
+            landed.wait_recv()
+        for copy, _ in self.copies:
+            copy.wait_send()
+
+
+def whole_kernel(
+    t_ref,
+    s_ref,
+    t_in,
+    t_bias,
+    t_out,
+    s_in,
+    s_bias,
+    s_out,
+    out_ref,
+    held,
+    x_t,
+    w1_hi,
+    w1_lo,
+    w2,
+    x,
+    bias,
+    acc,
+    edge,
+    edge_in,
+    section,
+    received,
+    w3,
+    w4,
+    x4,
+    acc4,
+    turned,
+    g_send,
+    g_recv,
+    e_send,
+    e_recv,
+    a_send,
+    a_recv,
+):
+    me = lax.axis_index("wide")
+    block = lax.axis_index("narrow")
+    gather = Gather(held, g_send, g_recv)
+    barrier = pltpu.get_barrier_semaphore()
+    above, below = (me, (block + 1) % 4), (me, (block + 3) % 4)
+    partners = gather.partners() + [above, below]
+    for partner in partners:
+        pl.semaphore_signal(barrier, inc=1, device_id=partner, device_id_type=MESH)
+    held[gather.at[0], gather.z, gather.at[1], gather.core] = t_ref[...]
+    x_t[...] = jnp.zeros_like(x_t)
+    pl.semaphore_wait(barrier, len(partners))
+
+    gather.first()
+    build_target_weights(t_in, t_out, w1_hi, w1_lo, w2)
+    gather.second()
+    build_source_weights(s_in, s_out, w3, w4)
+    gather.third()
+    gather.finish()
+
+    scale = s_ref.shape[-1] ** (-0.5)
+    product = lax.dot_general(
+        held[...].reshape(1024, 1024),
+        s_ref[...],
+        (((1,), (1,)), ((), ())),
+        preferred_element_type=F32,
+    )
+    cells = (product * scale).astype(BF16).astype(F32).reshape(128, 8, 128)
+    for l in range(128):
+        x_t[(l + 2) * 16 : (l + 2) * 16 + 8, :] = cells[l]
+
+    def row(slot):
+        return pl.ds(32 + slot, 128, stride=16)
+
+    copies = []
+    for n, (device, slots) in enumerate(((above, (6, 7)), (below, (0, 1)))):
+        for m, slot in enumerate(slots):
+            edge[n, m * 128 : (m + 1) * 128, :] = x_t[row(slot), :].astype(BF16)
+        copy = push(edge.at[n], edge_in.at[n], e_send.at[n], e_recv.at[n], device)
+        copy.start()
+        copies.append(copy)
+    for n, (inside, slots) in enumerate(((block > 0, (14, 15)), (block < 3, (8, 9)))):
+        copies[n].wait()
+        for m, slot in enumerate(slots):
+            value = edge_in[n, m * 128 : (m + 1) * 128, :].astype(F32)
+            x_t[row(slot), :] = jnp.where(inside, value, 0.0)
+
+    target_section(block, x_t, t_bias, w1_hi, w1_lo, w2, x, bias, acc, section)
+
+    def send(d, carry):
+        to = (me + d) % 64
+        start = pl.multiple_of(to * 16, 16)
+        push(
+            section.at[pl.ds(start, 16)], received.at[me], a_send, a_recv, (to, block)
+        ).start()
+        return carry
+
+    lax.fori_loop(1, 64, send, 0)
+    received[me] = section[pl.ds(pl.multiple_of(me * 16, 16), 16)]
+    everything = pltpu.make_async_copy(
+        received.at[0:63], received.at[0:63], a_recv
+    )
+    everything.wait()
+    source_section(received, s_bias, out_ref, w3, w4, x4, acc4, turned)
+    pltpu.make_async_copy(section.at[0:1008], section.at[0:1008], a_send).wait()
+
+
 VMEM = pl.BlockSpec(memory_space=pltpu.VMEM)
 SMEM = pl.BlockSpec(memory_space=pltpu.SMEM)
 
@@ -160,56 +375,46 @@
     source_in_bias,
     source_out_taps,
 ):
-    scale = source_features.shape[-1] ** (-0.5)
     local = jnp.swapaxes(target_features, 0, 1).reshape(16, 1024)
-    flat = lax.all_gather(local, "wide", axis=0, tiled=True)
-    product = jnp.dot(flat, source_features[0].T, preferred_element_type=F32) * scale
-    cells = product.astype(BF16).reshape(128, 8, 128)
-    up = [(i, i + 1) for i in range(3)]
-    down = [(i + 1, i) for i in range(3)]
-    below = lax.ppermute(cells[:, 6:8], "narrow", up)
-    above = lax.ppermute(cells[:, 0:2], "narrow", down)
-    gap = jnp.zeros((128, 4, 128), BF16)
-    x_t = jnp.concatenate([cells, above, gap, below], axis=1)
-    x_t = jnp.pad(x_t, ((2, 6), (0, 0), (0, 0))).reshape(136 * 16, 128)
-    section = pl.pallas_call(
-        target_kernel,
-        out_shape=jax.ShapeDtypeStruct((1024, 128), BF16),
-        in_specs=[VMEM] * 4,
+    return pl.pallas_call(
+        whole_kernel,
+        out_shape=jax.ShapeDtypeStruct((8, 2, 64, 128), BF16),
+        in_specs=[VMEM, VMEM, VMEM, VMEM, VMEM, SMEM, VMEM, SMEM],
         out_specs=VMEM,
         scratch_shapes=[
+            pltpu.VMEM((4, 2, 4, 2, 16, 1024), BF16),
+            pltpu.VMEM((136 * 16, 128), F32),
             pltpu.VMEM((256, 2304), BF16),
             pltpu.VMEM((256, 2304), BF16),
             pltpu.VMEM((2304, 256), BF16),
             pltpu.VMEM((1408, 256), BF16),
             pltpu.VMEM((11, 2304), F32),
             pltpu.VMEM((1408, 256), F32),
-        ],
-        compiler_params=pltpu.CompilerParams(vmem_limit_bytes=48 * 2**20),
-    )(
-        x_t,
-        jnp.tile(target_in_taps.T, (1, 16)),
-        jnp.tile(target_in_bias, 144)[None],
-        jnp.broadcast_to(target_out_taps.T[:, :, None], (9, 16, 128)),
-    )
-    received = lax.all_to_all(
-        section.reshape(64, 16, 128), "wide", split_axis=0, concat_axis=0, tiled=True
-    )
-    return pl.pallas_call(
-        source_kernel,
-        out_shape=jax.ShapeDtypeStruct((8, 2, 64, 128), BF16),
-        in_specs=[VMEM, SMEM, VMEM, SMEM],
-        out_specs=VMEM,
-        scratch_shapes=[
+            pltpu.VMEM((2, 256, 128), BF16),
+            pltpu.VMEM((2, 256, 128), BF16),
+            pltpu.VMEM((1024, 128), BF16),
+            pltpu.VMEM((64, 16, 128), BF16),
             pltpu.VMEM((8, 768, 256), BF16),
             pltpu.VMEM((8, 256, 768), BF16),
             pltpu.VMEM((1024, 768), BF16),
             pltpu.VMEM((1024, 384), F32),
             pltpu.VMEM((1024, 128), F32),
+            pltpu.SemaphoreType.DMA((63,)),
+            pltpu.SemaphoreType.DMA((63,)),
+            pltpu.SemaphoreType.DMA((2,)),
+            pltpu.SemaphoreType.DMA((2,)),
+            pltpu.SemaphoreType.DMA,
+            pltpu.SemaphoreType.DMA,
         ],
-        compiler_params=pltpu.CompilerParams(vmem_limit_bytes=48 * 2**20),
+        compiler_params=pltpu.CompilerParams(
+            collective_id=0, has_side_effects=True, vmem_limit_bytes=56 * 2**20
+        ),
     )(
-        received.reshape(1024, 128),
+        local,
+        source_features[0],
+        jnp.tile(target_in_taps.T, (1, 16)),
+        jnp.tile(target_in_bias, 144)[None],
+        jnp.broadcast_to(target_out_taps.T[:, :, None], (9, 16, 128)),
         source_in_taps,
         jnp.repeat(source_in_bias, 128)[None],
         source_out_taps,

time: 179 us -> 64.4 us (0.36)
  waiting for transfers between devices: 112 us -> 0 us
  Pallas kernels: 24.3 us -> 57.5 us
  blocking collectives: 17.3 us -> 0 us
  between operations: 13.5 us -> 0.02 us
  starting transfers between devices: 6.21 us -> 0 us
  local copies, waits for them, and re-layouts: 2.23 us -> 6.67 us
  matrix products: 2.3 us -> 0 us
    all_gather x1 -> x0, waiting for transfers between devices: 111 us -> none  [on_device(): flat = lax.all_gather(local, 'wide', axis=0, tiled=True)]
    pallas_call x2 -> x1, Pallas kernels: 24.3 us -> 57.5 us  [on_device(): pl.pallas_call(whole_kernel, out_shape=jax.ShapeDtypeStruct((8, 2, 64, 12...]
    all_to_all x1 -> x0, blocking collectives: 17.3 us -> none  [on_device(): lax.all_to_all(section.reshape(64, 16, 128), 'wide', split_axis=0, concat...]
    ppermute x2 -> x0, starting transfers between devices: 6.18 us -> none  [the longest x1 4.89 us: on_device(): below = lax.ppermute(cells[:, 6:8], 'narrow', up)]
    dot_general x1 -> x0, matrix products: 2.3 us -> none  [on_device(): jnp.dot(flat, source_features[0].T, preferred_element_type=F32) * scale]
  transfers between devices with their start and end apart: 3 -> 0, of which waited for: 2 -> 0; matrix products, arithmetic and copies ran while one was open for 0% -> 0% of each run, Pallas kernels for 0% -> 0%
where the time goes in v2:
time: 64.4 us; the launch traced here: 64.2 us
  Pallas kernels  57.5 us (89%)
  local copies, waits for them, and re-layouts  6.67 us (10%)
    pallas_call x1, Pallas kernels, on_device(): pl.pallas_call(whole_kernel, out_shape=jax.ShapeDtypeStruct((8, 2, 64, 12...  57.5 us
    unnamed x7, local copies, waits for them, and re-layouts  1.68 us

profile of v2, /device:TPU:1, one launch (start us, length us, event | category | flops | bytes accessed | tf_op | source)
XLA Modules:
  0.0 64.2 jit_solution(692189005295609353)
XLA Ops:
  0.0 0.0 copy-start
  0.0 0.8 %copy.13 = f32[9,16]{1,0:T(8,128)S(1)} copy(f32[9,16]{0,1:T(8,128)} %bitcast.12) | data formatting | bytes 1152 | tf_op jit(solution)/shard_map/transpose | solution.py:415
  0.8 0.0 copy-start.2
  0.8 0.8 %copy.14 = f32[9,16]{1,0:T(8,128)S(1)} copy(f32[9,16]{0,1:T(8,128)} %bitcast.13) | data formatting | bytes 1152 | tf_op jit(solution)/shard_map/transpose | solution.py:417
  1.6 0.0 copy-done.2
  1.6 0.7 %broadcast_in_dim.10 = f32[16,128]{1,0:T(8,128)} broadcast(f32[16]{0:T(128)S(1)} %copy-done.2), dimensions={0} | broadcast | bytes 8256 | tf_op jit(solution)/shard_map/broadcast_in_dim | solution.py:419
  2.3 0.0 copy-done
  2.3 0.6 copy.16
  2.9 0.7 %broadcast_in_dim.4.t_out = f32[9,16,128]{2,1,0:T(8,128)} broadcast(f32[9,16]{1,0:T(8,128)S(1)} %copy.14), dimensions={0,1} | broadcast | bytes 74304 | tf_op jit(solution)/shard_map/broadcast_in_dim | solution.py:417
  3.6 0.0 copy-start.1
  3.6 0.7 %tile.7.t_in = f32[9,256]{1,0:T(8,128)} reshape(f32[9,16,16]{2,1,0:T(8,128)S(1)} %tile.6) | data formatting | bytes 18432 | tf_op jit(solution)/shard_map/tile | solution.py:415
  4.3 0.0 copy-done.1
  4.3 0.7 %broadcast_in_dim_tile.3.t_bias = f32[1,2304]{1,0:T(1,128)} reshape(f32[144,16]{1,0:T(8,128)S(1)} %tile.8) | data formatting | bytes 18432 | tf_op jit(solution)/shard_map/broadcast_in_dim;tile | solution.py:416
  5.0 57.5 %shard_map.82 = bf16[8,2,64,128]{3,2,1,0:T(8,128)(2,1)} custom-call(bf16[16,1024]{1,0:T(8,128)(2,1)} %bitcast.9, bf16[128,1024]{1,0:T(8,128)(2,1)} %bitcast.8, f32[9,256]{1,0:T(8,128)} %tile.7.t_in, f32[1,2304]{1,0:T(1,128)} %broadcast_in_dim_tile.3.t_bias, f32[9,16,128]{2,1,0:T(8,128)} %broadcast_in_dim.4.t_out, f32[16,9]{1,0:T(8,128)} %s_in.1, ...), custom_call_target="tpu_custom_call" | custom-call | tf_op jit(solution)/shard_map/pallas_call | solution.py:379
  62.5 1.7 %copy.18 = bf16[8,2,64,128]{3,2,1,0:T(8,128)(2,1)} copy(bf16[8,2,64,128]{3,2,1,0:T(8,128)(2,1)} %shard_map.82) | data formatting | bytes 524288
  (2 shorter events, 0.0 us)
Async XLA Ops:
  0.0 2.3 %copy-start = (bf16[8,2,1024]{2,1,0:T(2,128)(2,1)S(1)}, bf16[8,2,1024]{2,1,0:T(2,128)(2,1)}, u32[]{:S(2)}) copy-start(bf16[8,2,1024]{2,1,0:T(2,128)(2,1)} %param.9) | copy-start | bytes 98308
  0.8 0.8 %copy-start.2 = (f32[16]{0:T(128)S(1)}, f32[16]{0:T(128)}, u32[]{:S(2)}) copy-start(f32[16]{0:T(128)} %param.14) | copy-start | bytes 196
  3.6 0.7 %copy-start.1 = (f32[16]{0:T(128)S(1)}, f32[16]{0:T(128)}, u32[]{:S(2)}) copy-start(f32[16]{0:T(128)} %param.11) | copy-start | bytes 196

commit v3 on v2

v3 whole, which is shorter than its diff:
```python
import functools

import jax
import jax.numpy as jnp
from jax import lax
from jax.experimental import pallas as pl
from jax.experimental.pallas import tpu as pltpu
from jax.sharding import PartitionSpec as P

F32 = jnp.float32
BF16 = jnp.bfloat16
OFF = -1e38


def split(value):
    high = value.astype(BF16)
    return high, (value - high.astype(F32)).astype(BF16)


def spread_taps(t_in, t_bias, t_out, in_rows, out_rows):
    lane = lax.broadcasted_iota(jnp.int32, (1, 256), 1) & 15
    row = lax.broadcasted_iota(jnp.int32, (16, 128), 0)
    for n in range(10):
        value = jnp.zeros((1, 256), F32)
        for h in range(16):
            value = jnp.where(lane == h, t_in[h, n] if n < 9 else t_bias[h], value)
        in_rows[n : n + 1, :] = value
    for n in range(9):
        value = jnp.zeros((16, 128), F32)
        for h in range(16):
            value = jnp.where(row == h, t_out[h, n], value)
        out_rows[n] = value


def build_target_weights(in_taps_ref, out_taps_ref, w1_hi, w1_lo, w2):
    def chunk(c, carry):
        shape = (256, 256)
        row = lax.broadcasted_iota(jnp.int32, shape, 0)
        cell = (lax.broadcasted_iota(jnp.int32, shape, 1) + c * 256) >> 4
        l_hid = (cell * 205) >> 11
        k_hid = cell - l_hid * 10
        code = ((row >> 4) - l_hid) * 16 + (((row & 15) - k_hid + 2) & 15)
        lanes = pl.ds(pl.multiple_of(c * 256, 256), 256)
        value = jnp.zeros(shape, F32)
        for a in range(3):
            for b in range(3):
                n = 3 * a + b
                taps = in_taps_ref[n : n + 1, :]
                value = jnp.where(code == b * 16 + a, taps, value)
        high, low = split(value)
        w1_hi[:, lanes] = high
        w1_lo[:, lanes] = low

        shape = (16, 1, 128)
        cell = lax.broadcasted_iota(jnp.int32, shape, 0) + c * 16
        lane = lax.broadcasted_iota(jnp.int32, shape, 2)
        l_hid = (cell * 205) >> 11
        k_hid = cell - l_hid * 10
        code = (l_hid - (lane >> 3)) * 16 + ((k_hid - (lane & 7)) & 15)
        code = jnp.broadcast_to(code, (16, 16, 128))
        value = jnp.zeros((16, 16, 128), F32)
        for a in range(3):
            for b in range(3):
                taps = out_taps_ref[3 * a + b]
                value = jnp.where(code == b * 16 + a, taps[None], value)
        high, low = split(value.reshape(256, 128))
        rows = pl.ds(pl.multiple_of(c * 256, 256), 256)
        w2[rows, 0:128] = high
        w2[rows, 128:256] = low
        return carry

    lax.fori_loop(0, 9, chunk, 0)


def target_section(block, x_t, bias_ref, w1_hi, w1_lo, w2, x, bias, acc):
    for p in range(11):
        part = x_t[p * 192 : p * 192 + 256, :]
        x[p * 128 : (p + 1) * 128, :] = part.T.astype(BF16)
    shape = (11, 2304)
    patch = lax.broadcasted_iota(jnp.int32, shape, 0)
    cell = lax.broadcasted_iota(jnp.int32, shape, 1) >> 4
    l_hid = (cell * 205) >> 11
    k_at = cell - l_hid * 10 - 1 + block * 8
    l_at = patch * 12 - 1 + l_hid
    valid = (l_at >= 0) & (l_at < 128) & (k_at >= 0) & (k_at < 32) & (cell < 140)
    spread = jnp.concatenate([bias_ref[9:10, :]] * 9, axis=1)
    bias[...] = jnp.where(valid, spread, OFF)

    acc[...] = jnp.zeros_like(acc)
    for c in range(9):
        lanes = slice(c * 256, (c + 1) * 256)
        hidden = jnp.dot(x[...], w1_hi[:, lanes], preferred_element_type=F32)
        hidden += jnp.dot(x[...], w1_lo[:, lanes], preferred_element_type=F32)
        hidden = hidden.reshape(11, 128, 256) + bias[:, lanes][:, None, :]
        hidden = jnp.maximum(hidden, 0.0).reshape(1408, 256)
        high, low = split(hidden)
        acc[...] += jnp.dot(high, w2[lanes, :], preferred_element_type=F32)
        acc[:, 0:128] += jnp.dot(low, w2[lanes, 0:128], preferred_element_type=F32)


def build_source_weights(in_taps, out_taps, w1, w2):
    def band(h, carry):
        shape = (128, 128)
        apart = lax.broadcasted_iota(jnp.int32, shape, 0) - lax.broadcasted_iota(
            jnp.int32, shape, 1
        )
        c, at = h // 2, pl.multiple_of((h % 2) * 128, 128)
        for a in range(3):
            for taps, w, first in ((in_taps, w1, True), (out_taps, w2, False)):
                value = jnp.zeros(shape, F32)
                for b in range(3):
                    value = jnp.where(apart == b - 1, taps[h, 3 * a + b], value)
                for n, part in enumerate(split(value)):
                    other = slice((3 * n + a) * 128, (3 * n + a + 1) * 128)
                    if first:
                        w[c, other, pl.ds(at, 128)] = part
                    else:
                        w[c, pl.ds(at, 128), other] = part
        return carry

    lax.fori_loop(0, 16, band, 0)


def source_section(r_ref, in_bias, out_ref, w1, w2, x, acc, turned):
    zero = jnp.zeros((16, 128), BF16)
    for n in range(2):
        at = n * 384
        x[0:16, at : at + 128] = zero
        x[16:1024, at : at + 128] = r_ref[0:63].reshape(1008, 128)
        x[:, at + 128 : at + 256] = r_ref[...].reshape(1024, 128)
        x[0:1008, at + 256 : at + 384] = r_ref[1:64].reshape(1008, 128)
        x[1008:1024, at + 256 : at + 384] = zero

    acc[...] = jnp.zeros_like(acc)
    lane = lax.broadcasted_iota(jnp.int32, (1, 256), 1)
    for c in range(8):
        hidden = jnp.dot(x[...], w1[c], preferred_element_type=F32)
        hidden = jnp.maximum(hidden + jnp.where(lane < 128, in_bias[2 * c], in_bias[2 * c + 1]), 0.0)
        high, low = split(hidden)
        both = jnp.dot(high, w2[c], preferred_element_type=F32)
        rest = jnp.dot(low, w2[c, :, 0:384], preferred_element_type=F32)
        acc[...] += both[:, 0:384] + both[:, 384:768] + rest
    for i in range(64):
        rows = slice(i * 16, (i + 1) * 16)
        total = acc[rows, 128:256]
        if i > 0:
            total += acc[i * 16 - 16 : i * 16, 0:128]
        if i < 63:
            total += acc[i * 16 + 16 : i * 16 + 32, 256:384]
        turned[pl.ds(i, 16, stride=64), :] = jnp.maximum(total, 0.0)
    for k in range(8):
        for l in range(2):
            n = l * 8 + k
            out_ref[k, l] = turned[n * 64 : (n + 1) * 64, :].astype(BF16)


MESH = pl.DeviceIdType.MESH


def push(src, dst, send_sem, recv_sem, device):
    return pltpu.make_async_remote_copy(
        src_ref=src,
        dst_ref=dst,
        send_sem=send_sem,
        recv_sem=recv_sem,
        device_id=device,
        device_id_type=MESH,
    )


class Gather:
    def __init__(self, held, send, recv):
        me = lax.axis_index("wide")
        self.narrow = lax.axis_index("narrow")
        self.held, self.send, self.recv = held, send, recv
        self.core = me % 2
        self.at = (me // 16, (me // 2) % 4)
        self.z = (me // 8) % 2
        self.count = 0
        self.copies = []

    def device(self, x=None, y=None, z=None, core=None, narrow=None):
        x = self.at[0] if x is None else x
        y = self.at[1] if y is None else y
        z = self.z if z is None else z
        core = self.core if core is None else core
        narrow = self.narrow if narrow is None else narrow
        return (((x * 2 + z) * 4 + y) * 2 + core, narrow)

    def along(self, half, d, other=0):
        n = (self.at[half] + d) % 4
        return self.device(z=(self.z + other) % 2, **{"xy"[half]: n})

    def partners(self):
        found = [self.device(core=1 - self.core)]
        for d, other in self.near():
            for half in range(2):
                if d > 0 or half == 0:
                    found.append(self.along(half, d, other))
        for step in (1, 3):
            for core in (self.core, 1 - self.core):
                found.append(self.device(core=core, narrow=(self.narrow + step) % 4))
        return found

    def near(self):
        return [(0, 1)] + [(d, other) for other in (0, 1) for d in (1, 3, 2)]

    def start(self, src, arrives, device):
        n = self.count
        self.count += 1
        copy = push(src, src, self.send.at[n], self.recv.at[n], device)
        copy.start()
        self.copies.append(copy)
        return push(src, arrives, self.send.at[n], self.recv.at[n], device)

    def back(self, half, steps):
        at = list(self.at)
        at[half] = (at[half] + 4 - steps) % 4
        return at

    def first(self):
        self.early, self.late = {}, {}
        for d, other in self.near():
            for half in range(2):
                lanes = slice(half * 512, half * 512 + 512)
                x, y = self.at
                src = self.held.at[x, self.z, y, :, lanes]
                x, y = self.back(half, d)
                landed = self.held.at[x, (self.z + other) % 2, y, :, lanes]
                self.early[half, d, other] = self.start(
                    src, landed, self.along(half, d, other)
                )

    def second(self):
        for e in (0, 1, 3, 2):
            for half in range(2):
                lanes = slice(half * 512, half * 512 + 512)
                for other in range(2):
                    if (e, other) != (0, 0):
                        self.early[half, e, other].wait_recv()
                at = self.back(half, e)
                x, y = at
                src = self.held.at[x, :, y, :, lanes]
                for d in (1, 3, 2):
                    x, y = at
                    if half == 0:
                        y = (y + 4 - d) % 4
                    else:
                        x = (x + 4 - d) % 4
                    landed = self.held.at[x, :, y, :, lanes]
                    self.late[half, e, d] = self.start(
                        src, landed, self.along(1 - half, d)
                    )

    def finish(self):
        for landed in self.late.values():
            landed.wait_recv()
        for copy in self.copies:
            copy.wait_send()


def whole_kernel(
    t_ref,
    s_ref,
    t_in,
    t_bias,
    t_out,
    s_in,
    s_bias,
    s_out,
    out_ref,
    held,
    x_t,
    w1_hi,
    w1_lo,
    w2,
    x,
    bias,
    acc,
    s_all,
    cells_f,
    cells_out,
    cells_in,
    edge,
    edge_in,
    section,
    received,
    w3,
    w4,
    x4,
    acc4,
    turned,
    in_rows,
    out_rows,
    g_send,
    g_recv,
    e_send,
    e_recv,
    a_send,
    a_recv,
):
    me = lax.axis_index("wide")
    block = lax.axis_index("narrow")
    gather = Gather(held, g_send, g_recv)
    core = gather.core
    barrier = pltpu.get_barrier_semaphore()
    partners = gather.partners()
    for partner in partners:
        pl.semaphore_signal(barrier, inc=1, device_id=partner, device_id_type=MESH)
    mine = t_ref[...].astype(F32)
    mine = jnp.concatenate([mine[:, 0, :], mine[:, 1, :]], axis=0)
    held[gather.at[0], gather.z, gather.at[1]] = mine.astype(BF16)
    s_all[0:128, :] = s_ref[...]
    x_t[...] = jnp.zeros_like(x_t)
    pl.semaphore_wait(barrier, len(partners))

    sibling = gather.device(core=1 - core)
    gather.first()
    other_row = push(s_ref, s_all.at[128:256], e_send.at[5], e_recv.at[5], sibling)
    other_row.start()
    spread_taps(t_in, t_bias, t_out, in_rows, out_rows)
    build_target_weights(in_rows, out_rows, w1_hi, w1_lo, w2)
    gather.second()
    build_source_weights(s_in, s_out, w3, w4)
    other_row.wait()
    gather.finish()

    scale = s_ref.shape[-1] ** (-0.5)
    product = lax.dot_general(
        held[...].reshape(512, 1024),
        s_all[...],
        (((1,), (1,)), ((), ())),
        preferred_element_type=F32,
    )
    product = (product * scale).astype(BF16)
    cells_f[0] = product[:, 0:128].astype(F32)
    cells_f[1] = product[:, 128:256].astype(F32)
    cells_out[...] = product[:, 128:256]
    copies = []
    n = 4
    copies.append(push(cells_out, cells_in, e_send.at[n], e_recv.at[n], sibling))
    copies[0].start()
    for up, slots in enumerate(((0, 1), (6, 7))):
        for away in range(2):
            n = up * 2 + away
            for m, slot in enumerate(slots):
                rows = cells_f[away, pl.ds(slot, 64, stride=8), :]
                edge[n, m * 64 : (m + 1) * 64, :] = rows.astype(BF16)
            device = gather.device(
                core=(core + away) % 2, narrow=(block + (1 if up else 3)) % 4
            )
            copy = push(edge.at[n], edge_in.at[n], e_send.at[n], e_recv.at[n], device)
            copy.start()
            copies.append(copy)

    def place(cells, core):
        for n in range(64):
            first = pl.multiple_of(32 + core * 32 + (n // 2) * 64 + (n % 2) * 16, 8)
            x_t[pl.ds(first, 8), :] = cells[n * 8 : n * 8 + 8]

    place(cells_f[0], core)
    for copy in copies:
        copy.wait()
    place(cells_in[...].astype(F32), 1 - core)
    for up, (inside, slots) in enumerate(((block < 3, (8, 9)), (block > 0, (14, 15)))):
        for away in range(2):
            at = (core + away) % 2
            for m, slot in enumerate(slots):
                value = edge_in[up * 2 + away, m * 64 : (m + 1) * 64, :].astype(F32)
                value = jnp.where(inside, value, 0.0)
                cells_f[away, 0:64, :] = value
                for l in range(2):
                    x_t[pl.ds(32 + at * 32 + l * 16 + slot, 32, stride=64), :] = cells_f[
                        away, pl.ds(l, 32, stride=2), :
                    ]

    target_section(block, x_t, in_rows, w1_hi, w1_lo, w2, x, bias, acc)

    def send(step, carry):
        p = (me // 6 + step) % 11
        rows = pl.ds(pl.multiple_of(p * 128, 128), 128)
        total = jnp.maximum(acc[rows, 0:128] + acc[rows, 128:256], 0.0).T
        section[pl.ds(pl.multiple_of(p * 96, 32), 96), :] = total[:96].astype(BF16)
        for q in range(6):
            to = p * 6 + q

            @pl.when((to < 64) & (to != me))
            def _():
                src = section.at[pl.ds(pl.multiple_of(to * 16, 16), 16)]
                push(src, received.at[me], a_send, a_recv, (to, block)).start()

        return carry

    lax.fori_loop(0, 11, send, 0)
    received[me] = section[pl.ds(pl.multiple_of(me * 16, 16), 16)]
    everything = pltpu.make_async_copy(
        received.at[0:63], received.at[0:63], a_recv
    )
    everything.wait()
    source_section(received, s_bias, out_ref, w3, w4, x4, acc4, turned)
    pltpu.make_async_copy(section.at[0:1008], section.at[0:1008], a_send).wait()


VMEM = pl.BlockSpec(memory_space=pltpu.VMEM)
SMEM = pl.BlockSpec(memory_space=pltpu.SMEM)


def on_device(
    source_features,
    target_features,
    target_in_taps,
    target_in_bias,
    target_out_taps,
    source_in_taps,
    source_in_bias,
    source_out_taps,
):
    return pl.pallas_call(
        whole_kernel,
        out_shape=jax.ShapeDtypeStruct((8, 2, 64, 128), BF16),
        in_specs=[VMEM, VMEM] + [SMEM] * 6,
        out_specs=VMEM,
        scratch_shapes=[
            pltpu.VMEM((4, 2, 4, 16, 1024), BF16),
            pltpu.VMEM((136 * 16, 128), F32),
            pltpu.VMEM((256, 2304), BF16),
            pltpu.VMEM((256, 2304), BF16),
            pltpu.VMEM((2304, 256), BF16),
            pltpu.VMEM((1408, 256), BF16),
            pltpu.VMEM((11, 2304), F32),
            pltpu.VMEM((1408, 256), F32),
            pltpu.VMEM((256, 1024), BF16),
            pltpu.VMEM((2, 512, 128), F32),
            pltpu.VMEM((512, 128), BF16),
            pltpu.VMEM((512, 128), BF16),
            pltpu.VMEM((4, 128, 128), BF16),
            pltpu.VMEM((4, 128, 128), BF16),
            pltpu.VMEM((1056, 128), BF16),
            pltpu.VMEM((64, 16, 128), BF16),
            pltpu.VMEM((8, 768, 256), BF16),
            pltpu.VMEM((8, 256, 768), BF16),
            pltpu.VMEM((1024, 768), BF16),
            pltpu.VMEM((1024, 384), F32),
            pltpu.VMEM((1024, 128), F32),
            pltpu.VMEM((16, 256), F32),
            pltpu.VMEM((9, 16, 128), F32),
            pltpu.SemaphoreType.DMA((38,)),
            pltpu.SemaphoreType.DMA((38,)),
            pltpu.SemaphoreType.DMA((6,)),
            pltpu.SemaphoreType.DMA((6,)),
            pltpu.SemaphoreType.DMA,
            pltpu.SemaphoreType.DMA,
        ],
        compiler_params=pltpu.CompilerParams(
            collective_id=0, has_side_effects=True, vmem_limit_bytes=56 * 2**20
        ),
    )(
        target_features,
        source_features[0],
        target_in_taps,
        target_in_bias,
        target_out_taps,
        source_in_taps,
        source_in_bias,
        source_out_taps,
    )


def solution(mesh):
    placed = (P("wide", None, None), P("narrow", "wide", None), P(), P(), P(), P(), P(), P())
    return jax.shard_map(
        on_device,
        mesh=mesh,
        in_specs=placed,
        out_specs=P("narrow", "wide", None, None),
        check_vma=False,
    )
```

time: 64.4 us -> 55.9 us (0.87)
  local copies, waits for them, and re-layouts: 6.67 us -> 1.67 us
  Pallas kernels: 57.5 us -> 54.1 us
    pallas_call x1, Pallas kernels: 57.5 us -> 54.1 us  [on_device(): pl.pallas_call(whole_kernel, out_shape=jax.ShapeDtypeStruct((8, 2, 64, 12...]
    transpose x3 -> x0, local copies, waits for them, and re-layouts: 2.2 us -> none  [the longest x1 0.79 us: on_device(): target_out_taps.T[:, :, None]]
    another operation x4 -> x0, local copies, waits for them, and re-layouts: 1.4 us -> none  [the longest x2 0.7 us: on_device(): jnp.tile(target_in_bias, 144)[None]]
    broadcast_in_dim x2 -> x0, local copies, waits for them, and re-layouts: 1.38 us -> none  [the longest x1 0.72 us: on_device(): jnp.broadcast_to(target_out_taps.T[:, :, None], (9, 16, 128))]
    unnamed x7 -> x1, local copies, waits for them, and re-layouts: 1.68 us -> 1.67 us
where the time goes in v3:
time: 55.9 us; the launch traced here: 55.7 us
  Pallas kernels  54.1 us (97%)
  local copies, waits for them, and re-layouts  1.67 us (3%)
    pallas_call x1, Pallas kernels, on_device(): pl.pallas_call(whole_kernel, out_shape=jax.ShapeDtypeStruct((8, 2, 64, 12...  54.1 us
    unnamed x1, local copies, waits for them, and re-layouts  1.67 us

profile of v3, /device:TPU:1, one launch (start us, length us, event | category | flops | bytes accessed | tf_op | source)
XLA Modules:
  0.0 55.7 jit_solution(9580857283405587024)
XLA Ops:
  0.0 54.1 %shard_map.82 = bf16[8,2,64,128]{3,2,1,0:T(8,128)(2,1)} custom-call(bf16[8,2,1024]{2,1,0:T(2,128)(2,1)} %t_ref.1, bf16[128,1024]{1,0:T(8,128)(2,1)} %bitcast.1, f32[16,9]{1,0:T(8,128)} %t_in.1, f32[16]{0:T(128)} %t_bias.1, f32[16,9]{1,0:T(8,128)} %t_out.1, f32[16,9]{1,0:T(8,128)} %s_in.1, f32[16]{0:T(128)} %s_bias.1, f32[16,9]{1,0:T(8,128)} %s_out.1), custom_call_target="tpu_custom_call" | custom-call | tf_op jit(solution)/shard_map/pallas_call | solution.py:418
  54.1 1.7 %copy.10 = bf16[8,2,64,128]{3,2,1,0:T(8,128)(2,1)} copy(bf16[8,2,64,128]{3,2,1,0:T(8,128)(2,1)} %shard_map.82) | data formatting | bytes 524288

commit v4 on v3

--- a/solution.py
+++ b/solution.py
@@ -32,38 +32,44 @@
         out_rows[n] = value
 
 
-def build_target_weights(in_taps_ref, out_taps_ref, w1_hi, w1_lo, w2):
+def place_of(cell):
+    inner = (cell * 171) >> 10
+    rest = cell - 84
+    l_edge, k_edge = rest >> 2, rest & 3
+    l_hid = jnp.where(cell < 84, inner, l_edge)
+    k_hid = jnp.where(cell < 84, cell - inner * 6 + 2, jnp.where(k_edge < 2, k_edge, k_edge + 6))
+    return l_hid, k_hid
+
+
+def chosen(code, taps):
+    value = jnp.zeros(code.shape, F32)
+    for a in range(3):
+        for b in range(3):
+            value = jnp.where(code == b * 16 + a, taps(3 * a + b), value)
+    return value
+
+
+def build_target_weights(in_taps_ref, out_taps_ref, w1, wh, w2):
+    def taps_in(n):
+        return in_taps_ref[n : n + 1, :]
+
     def chunk(c, carry):
-        shape = (256, 256)
+        shape = (128, 256)
         row = lax.broadcasted_iota(jnp.int32, shape, 0)
-        cell = (lax.broadcasted_iota(jnp.int32, shape, 1) + c * 256) >> 4
-        l_hid = (cell * 205) >> 11
-        k_hid = cell - l_hid * 10
-        code = ((row >> 4) - l_hid) * 16 + (((row & 15) - k_hid + 2) & 15)
+        cell = (lax.broadcasted_iota(jnp.int32, (1, 256), 1) + c * 256) >> 4
+        l_hid, k_hid = place_of(cell)
+        code = ((row >> 3) - l_hid) * 16 + (((row & 7) - k_hid + 2) & 15)
         lanes = pl.ds(pl.multiple_of(c * 256, 256), 256)
-        value = jnp.zeros(shape, F32)
-        for a in range(3):
-            for b in range(3):
-                n = 3 * a + b
-                taps = in_taps_ref[n : n + 1, :]
-                value = jnp.where(code == b * 16 + a, taps, value)
-        high, low = split(value)
-        w1_hi[:, lanes] = high
-        w1_lo[:, lanes] = low
-
-        shape = (16, 1, 128)
-        cell = lax.broadcasted_iota(jnp.int32, shape, 0) + c * 16
-        lane = lax.broadcasted_iota(jnp.int32, shape, 2)
-        l_hid = (cell * 205) >> 11
-        k_hid = cell - l_hid * 10
+        high, low = split(chosen(code, taps_in))
+        w1[0:128, lanes] = high
+        w1[128:256, lanes] = low
+
+        cell = lax.broadcasted_iota(jnp.int32, (16, 1, 128), 0) + c * 16
+        lane = lax.broadcasted_iota(jnp.int32, (16, 1, 128), 2)
+        l_hid, k_hid = place_of(cell)
         code = (l_hid - (lane >> 3)) * 16 + ((k_hid - (lane & 7)) & 15)
         code = jnp.broadcast_to(code, (16, 16, 128))
-        value = jnp.zeros((16, 16, 128), F32)
-        for a in range(3):
-            for b in range(3):
-                taps = out_taps_ref[3 * a + b]
-                value = jnp.where(code == b * 16 + a, taps[None], value)
-        high, low = split(value.reshape(256, 128))
+        high, low = split(chosen(code, lambda n: out_taps_ref[n][None]).reshape(256, 128))
         rows = pl.ds(pl.multiple_of(c * 256, 256), 256)
         w2[rows, 0:128] = high
         w2[rows, 128:256] = low
@@ -71,31 +77,52 @@
 
     lax.fori_loop(0, 9, chunk, 0)
 
-
-def target_section(block, x_t, bias_ref, w1_hi, w1_lo, w2, x, bias, acc):
-    for p in range(11):
-        part = x_t[p * 192 : p * 192 + 256, :]
-        x[p * 128 : (p + 1) * 128, :] = part.T.astype(BF16)
+    def edge_chunk(c, carry):
+        row = lax.broadcasted_iota(jnp.int32, (64, 256), 0)
+        cell = (lax.broadcasted_iota(jnp.int32, (1, 256), 1) + c * 256 + 1280) >> 4
+        l_hid, k_hid = place_of(cell)
+        m = row & 3
+        k_in = jnp.where(m < 2, m - 2, m + 6)
+        code = ((row >> 2) - l_hid) * 16 + ((k_in - k_hid + 2) & 15)
+        lanes = pl.ds(pl.multiple_of(c * 256, 256), 256)
+        high, low = split(chosen(code, taps_in))
+        wh[0:64, lanes] = high
+        wh[64:128, lanes] = low
+        return carry
+
+    lax.fori_loop(0, 4, edge_chunk, 0)
+
+
+def target_bias(block, first, spread_ref, bias):
     shape = (11, 2304)
-    patch = lax.broadcasted_iota(jnp.int32, shape, 0)
-    cell = lax.broadcasted_iota(jnp.int32, shape, 1) >> 4
-    l_hid = (cell * 205) >> 11
-    k_at = cell - l_hid * 10 - 1 + block * 8
+    patch = lax.broadcasted_iota(jnp.int32, shape, 0) + first
+    patch = jnp.where(patch >= 11, patch - 11, patch)
+    cell = lax.broadcasted_iota(jnp.int32, (1, 2304), 1) >> 4
+    l_hid, k_hid = place_of(cell)
+    k_at = k_hid - 1 + block * 8
     l_at = patch * 12 - 1 + l_hid
     valid = (l_at >= 0) & (l_at < 128) & (k_at >= 0) & (k_at < 32) & (cell < 140)
-    spread = jnp.concatenate([bias_ref[9:10, :]] * 9, axis=1)
+    spread = jnp.concatenate([spread_ref[9:10, :]] * 9, axis=1)
     bias[...] = jnp.where(valid, spread, OFF)
 
-    acc[...] = jnp.zeros_like(acc)
-    for c in range(9):
-        lanes = slice(c * 256, (c + 1) * 256)
-        hidden = jnp.dot(x[...], w1_hi[:, lanes], preferred_element_type=F32)
-        hidden += jnp.dot(x[...], w1_lo[:, lanes], preferred_element_type=F32)
-        hidden = hidden.reshape(11, 128, 256) + bias[:, lanes][:, None, :]
-        hidden = jnp.maximum(hidden, 0.0).reshape(1408, 256)
-        high, low = split(hidden)
-        acc[...] += jnp.dot(high, w2[lanes, :], preferred_element_type=F32)
-        acc[:, 0:128] += jnp.dot(low, w2[lanes, 0:128], preferred_element_type=F32)
+
+def target_chunk(c, steps, x, xh, bias, w1, wh, w2, acc):
+    rows = slice(steps.start * 128, steps.stop * 128)
+    count = steps.stop - steps.start
+    lanes = slice(c * 256, (c + 1) * 256)
+    hidden = jnp.dot(x[rows, :], w1[:, lanes], preferred_element_type=F32)
+    if c >= 5:
+        edge_lanes = slice(c * 256 - 1280, c * 256 - 1024)
+        hidden += jnp.dot(xh[rows, :], wh[:, edge_lanes], preferred_element_type=F32)
+    hidden = hidden.reshape(count, 128, 256) + bias[steps, lanes][:, None, :]
+    high, low = split(jnp.maximum(hidden, 0.0).reshape(count * 128, 256))
+    first = jnp.dot(high, w2[lanes, :], preferred_element_type=F32)
+    rest = jnp.dot(low, w2[lanes, 0:128], preferred_element_type=F32)
+    if c == 0:
+        acc[rows, :] = first
+    else:
+        acc[rows, :] += first
+    acc[rows, 0:128] += rest
 
 
 def build_source_weights(in_taps, out_taps, w1, w2):
@@ -271,10 +298,12 @@
     out_ref,
     held,
     x_t,
-    w1_hi,
-    w1_lo,
+    xh_t,
+    w1,
+    wh,
     w2,
     x,
+    xh,
     bias,
     acc,
     s_all,
@@ -312,6 +341,7 @@
     held[gather.at[0], gather.z, gather.at[1]] = mine.astype(BF16)
     s_all[0:128, :] = s_ref[...]
     x_t[...] = jnp.zeros_like(x_t)
+    xh_t[...] = jnp.zeros_like(xh_t)
     pl.semaphore_wait(barrier, len(partners))
 
     sibling = gather.device(core=1 - core)
@@ -319,7 +349,8 @@
     other_row = push(s_ref, s_all.at[128:256], e_send.at[5], e_recv.at[5], sibling)
     other_row.start()
     spread_taps(t_in, t_bias, t_out, in_rows, out_rows)
-    build_target_weights(in_rows, out_rows, w1_hi, w1_lo, w2)
+    build_target_weights(in_rows, out_rows, w1, wh, w2)
+    target_bias(block, me // 6, in_rows, bias)
     gather.second()
     build_source_weights(s_in, s_out, w3, w4)
     other_row.wait()
@@ -355,14 +386,25 @@
 
     def place(cells, core):
         for n in range(64):
-            first = pl.multiple_of(32 + core * 32 + (n // 2) * 64 + (n % 2) * 16, 8)
+            first = pl.multiple_of(16 + core * 16 + (n // 2) * 32 + (n % 2) * 8, 8)
             x_t[pl.ds(first, 8), :] = cells[n * 8 : n * 8 + 8]
 
+    patches = [(me // 6 + step) % 11 for step in range(11)]
     place(cells_f[0], core)
-    for copy in copies:
+    copies[0].wait()
+    place(cells_in[...].astype(F32), 1 - core)
+    for step, p in enumerate(patches):
+        turned_part = x_t[pl.ds(pl.multiple_of(p * 96, 32), 128), :].T.astype(BF16)
+        x[step * 128 : step * 128 + 128, 0:128] = turned_part
+        x[step * 128 : step * 128 + 128, 128:256] = turned_part
+
+    every = slice(0, 11)
+    for c in range(5):
+        target_chunk(c, every, x, xh, bias, w1, wh, w2, acc)
+
+    for copy in copies[1:]:
         copy.wait()
-    place(cells_in[...].astype(F32), 1 - core)
-    for up, (inside, slots) in enumerate(((block < 3, (8, 9)), (block > 0, (14, 15)))):
+    for up, (inside, slots) in enumerate(((block < 3, (2, 3)), (block > 0, (0, 1)))):
         for away in range(2):
             at = (core + away) % 2
             for m, slot in enumerate(slots):
@@ -370,28 +412,32 @@
                 value = jnp.where(inside, value, 0.0)
                 cells_f[away, 0:64, :] = value
                 for l in range(2):
-                    x_t[pl.ds(32 + at * 32 + l * 16 + slot, 32, stride=64), :] = cells_f[
+                    xh_t[pl.ds(8 + at * 8 + l * 4 + slot, 32, stride=16), :] = cells_f[
                         away, pl.ds(l, 32, stride=2), :
                     ]
-
-    target_section(block, x_t, in_rows, w1_hi, w1_lo, w2, x, bias, acc)
-
-    def send(step, carry):
-        p = (me // 6 + step) % 11
-        rows = pl.ds(pl.multiple_of(p * 128, 128), 128)
-        total = jnp.maximum(acc[rows, 0:128] + acc[rows, 128:256], 0.0).T
-        section[pl.ds(pl.multiple_of(p * 96, 32), 96), :] = total[:96].astype(BF16)
-        for q in range(6):
-            to = p * 6 + q
-
-            @pl.when((to < 64) & (to != me))
-            def _():
-                src = section.at[pl.ds(pl.multiple_of(to * 16, 16), 16)]
-                push(src, received.at[me], a_send, a_recv, (to, block)).start()
-
-        return carry
-
-    lax.fori_loop(0, 11, send, 0)
+    for step, p in enumerate(patches):
+        turned_part = xh_t[pl.ds(pl.multiple_of(p * 48, 16), 64), :].T.astype(BF16)
+        xh[step * 128 : step * 128 + 128, :] = jnp.concatenate(
+            [turned_part, turned_part], axis=1
+        )
+
+    for steps in (slice(0, 6), slice(6, 11)):
+        for c in range(5, 9):
+            target_chunk(c, steps, x, xh, bias, w1, wh, w2, acc)
+        for step in range(steps.start, steps.stop):
+            p = patches[step]
+            rows = slice(step * 128, step * 128 + 128)
+            total = jnp.maximum(acc[rows, 0:128] + acc[rows, 128:256], 0.0).T
+            section[pl.ds(pl.multiple_of(p * 96, 32), 96), :] = total[:96].astype(BF16)
+        for step in range(steps.start, steps.stop):
+            for q in range(6):
+                to = patches[step] * 6 + q
+
+                @pl.when((to < 64) & (to != me))
+                def _():
+                    src = section.at[pl.ds(pl.multiple_of(to * 16, 16), 16)]
+                    push(src, received.at[me], a_send, a_recv, (to, block)).start()
+
     received[me] = section[pl.ds(pl.multiple_of(me * 16, 16), 16)]
     everything = pltpu.make_async_copy(
         received.at[0:63], received.at[0:63], a_recv
@@ -422,11 +468,13 @@
         out_specs=VMEM,
         scratch_shapes=[
             pltpu.VMEM((4, 2, 4, 16, 1024), BF16),
-            pltpu.VMEM((136 * 16, 128), F32),
+            pltpu.VMEM((136 * 8, 128), F32),
+            pltpu.VMEM((136 * 4, 128), F32),
             pltpu.VMEM((256, 2304), BF16),
-            pltpu.VMEM((256, 2304), BF16),
+            pltpu.VMEM((128, 1024), BF16),
             pltpu.VMEM((2304, 256), BF16),
             pltpu.VMEM((1408, 256), BF16),
+            pltpu.VMEM((1408, 128), BF16),
             pltpu.VMEM((11, 2304), F32),
             pltpu.VMEM((1408, 256), F32),
             pltpu.VMEM((256, 1024), BF16),

time: 55.9 us -> 50.9 us (0.911)
  Pallas kernels: 54.1 us -> 49.1 us
    pallas_call x1, Pallas kernels: 54.1 us -> 49.1 us  [on_device(): pl.pallas_call(whole_kernel, out_shape=jax.ShapeDtypeStruct((8, 2, 64, 12...]
where the time goes in v4:
time: 50.9 us; the launch traced here: 50.8 us
  Pallas kernels  49.1 us (96%)
  local copies, waits for them, and re-layouts  1.67 us (3%)
    pallas_call x1, Pallas kernels, on_device(): pl.pallas_call(whole_kernel, out_shape=jax.ShapeDtypeStruct((8, 2, 64, 12...  49.1 us
    unnamed x1, local copies, waits for them, and re-layouts  1.67 us

profile of v4, /device:TPU:1, one launch (start us, length us, event | category | flops | bytes accessed | tf_op | source)
XLA Modules:
  0.0 50.8 jit_solution(6022494962343850287)
XLA Ops:
  0.0 49.1 %shard_map.82 = bf16[8,2,64,128]{3,2,1,0:T(8,128)(2,1)} custom-call(bf16[8,2,1024]{2,1,0:T(2,128)(2,1)} %t_ref.1, bf16[128,1024]{1,0:T(8,128)(2,1)} %bitcast.1, f32[16,9]{1,0:T(8,128)} %t_in.1, f32[16]{0:T(128)} %t_bias.1, f32[16,9]{1,0:T(8,128)} %t_out.1, f32[16,9]{1,0:T(8,128)} %s_in.1, f32[16]{0:T(128)} %s_bias.1, f32[16,9]{1,0:T(8,128)} %s_out.1), custom_call_target="tpu_custom_call" | custom-call | tf_op jit(solution)/shard_map/pallas_call | solution.py:464
  49.1 1.7 %copy.10 = bf16[8,2,64,128]{3,2,1,0:T(8,128)(2,1)} copy(bf16[8,2,64,128]{3,2,1,0:T(8,128)(2,1)} %shard_map.82) | data formatting | bytes 524288

commit v5 on v4

--- a/solution.py
+++ b/solution.py
@@ -148,37 +148,37 @@
     lax.fori_loop(0, 16, band, 0)
 
 
-def source_section(r_ref, in_bias, out_ref, w1, w2, x, acc, turned):
-    zero = jnp.zeros((16, 128), BF16)
-    for n in range(2):
-        at = n * 384
-        x[0:16, at : at + 128] = zero
-        x[16:1024, at : at + 128] = r_ref[0:63].reshape(1008, 128)
-        x[:, at + 128 : at + 256] = r_ref[...].reshape(1024, 128)
-        x[0:1008, at + 256 : at + 384] = r_ref[1:64].reshape(1008, 128)
-        x[1008:1024, at + 256 : at + 384] = zero
-
-    acc[...] = jnp.zeros_like(acc)
+def source_section(r_ref, in_bias, out_ref, w1, w2, acc, turned):
     lane = lax.broadcasted_iota(jnp.int32, (1, 256), 1)
-    for c in range(8):
-        hidden = jnp.dot(x[...], w1[c], preferred_element_type=F32)
-        hidden = jnp.maximum(hidden + jnp.where(lane < 128, in_bias[2 * c], in_bias[2 * c + 1]), 0.0)
-        high, low = split(hidden)
+
+    def chunk(c, first, count):
+        near = [r_ref[first + a : first + a + count].reshape(count * 16, 128) for a in range(3)]
+        rows = slice(first * 16, (first + count) * 16)
+        spread = jnp.where(lane < 128, in_bias[2 * c], in_bias[2 * c + 1])
+        hidden = jnp.dot(
+            jnp.concatenate(near + near, axis=1), w1[c], preferred_element_type=F32
+        )
+        high, low = split(jnp.maximum(hidden + spread, 0.0))
         both = jnp.dot(high, w2[c], preferred_element_type=F32)
         rest = jnp.dot(low, w2[c, :, 0:384], preferred_element_type=F32)
-        acc[...] += both[:, 0:384] + both[:, 384:768] + rest
-    for i in range(64):
-        rows = slice(i * 16, (i + 1) * 16)
-        total = acc[rows, 128:256]
-        if i > 0:
-            total += acc[i * 16 - 16 : i * 16, 0:128]
-        if i < 63:
-            total += acc[i * 16 + 16 : i * 16 + 32, 256:384]
-        turned[pl.ds(i, 16, stride=64), :] = jnp.maximum(total, 0.0)
-    for k in range(8):
-        for l in range(2):
-            n = l * 8 + k
-            out_ref[k, l] = turned[n * 64 : (n + 1) * 64, :].astype(BF16)
+        total = both[:, 0:384] + both[:, 384:768] + rest
+        acc[rows, :] = total if c == 0 else acc[rows, :] + total
+
+    def finish(rows):
+        for i in rows:
+            total = acc[i * 16 : i * 16 + 16, 128:256]
+            if i > 0:
+                total += acc[i * 16 - 16 : i * 16, 0:128]
+            if i < 63:
+                total += acc[i * 16 + 16 : i * 16 + 32, 256:384]
+            out_ref[i] = jnp.maximum(total, 0.0).astype(BF16)
+
+    for c in range(7):
+        chunk(c, 0, 64)
+    chunk(7, 0, 32)
+    finish(range(0, 31))
+    chunk(7, 32, 32)
+    finish(range(31, 64))
 
 
 MESH = pl.DeviceIdType.MESH
@@ -287,15 +287,23 @@
 
 
 def whole_kernel(
+    t_given,
+    s_given,
+    t_in_given,
+    t_bias_given,
+    t_out_given,
+    s_in_given,
+    s_bias_given,
+    s_out_given,
+    out_ref,
     t_ref,
-    s_ref,
     t_in,
     t_bias,
     t_out,
     s_in,
     s_bias,
     s_out,
-    out_ref,
+    given_sem,
     held,
     x_t,
     xh_t,
@@ -316,7 +324,6 @@
     received,
     w3,
     w4,
-    x4,
     acc4,
     turned,
     in_rows,
@@ -336,17 +343,38 @@
     partners = gather.partners()
     for partner in partners:
         pl.semaphore_signal(barrier, inc=1, device_id=partner, device_id_type=MESH)
+    loads = [
+        pltpu.make_async_copy(src, dst, given_sem.at[n])
+        for n, (src, dst) in enumerate(
+            (
+                (t_given, t_ref),
+                (s_given, s_all.at[0:128]),
+                (t_in_given, t_in),
+                (t_bias_given, t_bias),
+                (t_out_given, t_out),
+                (s_in_given, s_in),
+                (s_bias_given, s_bias),
+                (s_out_given, s_out),
+            )
+        )
+    ]
+    for load in loads:
+        load.start()
+    x_t[...] = jnp.zeros_like(x_t)
+    xh_t[...] = jnp.zeros_like(xh_t)
+    for n in (0, 65):
+        received[n] = jnp.zeros((16, 128), BF16)
+    loads[0].wait()
     mine = t_ref[...].astype(F32)
     mine = jnp.concatenate([mine[:, 0, :], mine[:, 1, :]], axis=0)
     held[gather.at[0], gather.z, gather.at[1]] = mine.astype(BF16)
-    s_all[0:128, :] = s_ref[...]
-    x_t[...] = jnp.zeros_like(x_t)
-    xh_t[...] = jnp.zeros_like(xh_t)
+    for load in loads[1:]:
+        load.wait()
     pl.semaphore_wait(barrier, len(partners))
 
     sibling = gather.device(core=1 - core)
     gather.first()
-    other_row = push(s_ref, s_all.at[128:256], e_send.at[5], e_recv.at[5], sibling)
+    other_row = push(s_all.at[0:128], s_all.at[128:256], e_send.at[5], e_recv.at[5], sibling)
     other_row.start()
     spread_taps(t_in, t_bias, t_out, in_rows, out_rows)
     build_target_weights(in_rows, out_rows, w1, wh, w2)
@@ -356,7 +384,7 @@
     other_row.wait()
     gather.finish()
 
-    scale = s_ref.shape[-1] ** (-0.5)
+    scale = s_all.shape[-1] ** (-0.5)
     product = lax.dot_general(
         held[...].reshape(512, 1024),
         s_all[...],
@@ -436,19 +464,18 @@
                 @pl.when((to < 64) & (to != me))
                 def _():
                     src = section.at[pl.ds(pl.multiple_of(to * 16, 16), 16)]
-                    push(src, received.at[me], a_send, a_recv, (to, block)).start()
-
-    received[me] = section[pl.ds(pl.multiple_of(me * 16, 16), 16)]
+                    push(src, received.at[me + 1], a_send, a_recv, (to, block)).start()
+
+    received[me + 1] = section[pl.ds(pl.multiple_of(me * 16, 16), 16)]
     everything = pltpu.make_async_copy(
         received.at[0:63], received.at[0:63], a_recv
     )
     everything.wait()
-    source_section(received, s_bias, out_ref, w3, w4, x4, acc4, turned)
+    source_section(received, s_bias, out_ref, w3, w4, acc4, turned)
     pltpu.make_async_copy(section.at[0:1008], section.at[0:1008], a_send).wait()
 
 
 VMEM = pl.BlockSpec(memory_space=pltpu.VMEM)
-SMEM = pl.BlockSpec(memory_space=pltpu.SMEM)
 
 
 def on_device(
@@ -461,12 +488,20 @@
     source_in_bias,
     source_out_taps,
 ):
-    return pl.pallas_call(
+    result = pl.pallas_call(
         whole_kernel,
-        out_shape=jax.ShapeDtypeStruct((8, 2, 64, 128), BF16),
-        in_specs=[VMEM, VMEM] + [SMEM] * 6,
+        out_shape=pltpu.VMEM((64, 16, 128), BF16),
+        in_specs=[pl.BlockSpec(memory_space=pl.ANY)] * 8,
         out_specs=VMEM,
         scratch_shapes=[
+            pltpu.VMEM((8, 2, 1024), BF16),
+            pltpu.SMEM((16, 9), F32),
+            pltpu.SMEM((16,), F32),
+            pltpu.SMEM((16, 9), F32),
+            pltpu.SMEM((16, 9), F32),
+            pltpu.SMEM((16,), F32),
+            pltpu.SMEM((16, 9), F32),
+            pltpu.SemaphoreType.DMA((8,)),
             pltpu.VMEM((4, 2, 4, 16, 1024), BF16),
             pltpu.VMEM((136 * 8, 128), F32),
             pltpu.VMEM((136 * 4, 128), F32),
@@ -484,10 +519,9 @@
             pltpu.VMEM((4, 128, 128), BF16),
             pltpu.VMEM((4, 128, 128), BF16),
             pltpu.VMEM((1056, 128), BF16),
-            pltpu.VMEM((64, 16, 128), BF16),
+            pltpu.VMEM((66, 16, 128), BF16),
             pltpu.VMEM((8, 768, 256), BF16),
             pltpu.VMEM((8, 256, 768), BF16),
-            pltpu.VMEM((1024, 768), BF16),
             pltpu.VMEM((1024, 384), F32),
             pltpu.VMEM((1024, 128), F32),
             pltpu.VMEM((16, 256), F32),
@@ -512,6 +546,7 @@
         source_in_bias,
         source_out_taps,
     )
+    return jnp.transpose(result.reshape(64, 2, 8, 128), (2, 1, 0, 3))
 
 
 def solution(mesh):

time: 50.9 us -> 48 us (0.943)
  Pallas kernels: 49.1 us -> 47.1 us
  local copies, waits for them, and re-layouts: 1.67 us -> 0.77 us
    pallas_call x1, Pallas kernels: 49.1 us -> 47.1 us  [on_device(): pl.pallas_call(whole_kernel, out_shape=pltpu.VMEM((64, 16, 128), BF16), i...]
    unnamed x1 -> x0, local copies, waits for them, and re-layouts: 1.67 us -> none
    reshape x0 -> x1, local copies, waits for them, and re-layouts: none -> 0.77 us  [on_device(): return jnp.transpose(result.reshape(64, 2, 8, 128), (2, 1, 0, 3))]
where the time goes in v5:
time: 48 us; the launch traced here: 47.9 us
  Pallas kernels  47.1 us (98%)
  local copies, waits for them, and re-layouts  0.77 us (2%)
    pallas_call x1, Pallas kernels, on_device(): pl.pallas_call(whole_kernel, out_shape=pltpu.VMEM((64, 16, 128), BF16), i...  47.1 us

profile of v5, /device:TPU:1, one launch (start us, length us, event | category | flops | bytes accessed | tf_op | source)
XLA Modules:
  0.0 47.9 jit_solution(780296855797611400)
XLA Ops:
  0.0 47.1 %shard_map.82 = bf16[64,16,128]{2,1,0:T(8,128)(2,1)S(1)} custom-call(bf16[8,2,1024]{2,1,0:T(2,128)(2,1)} %t_given.1, bf16[128,1024]{1,0:T(8,128)(2,1)} %bitcast.6, f32[16,9]{1,0:T(8,128)} %t_in_given.1, f32[16]{0:T(128)} %t_bias_given.1, f32[16,9]{1,0:T(8,128)} %t_out_given.1, f32[16,9]{1,0:T(8,128)} %s_in_given.1, f32[16]{0:T(128)} %s_bias_given.1, ...), custom_call_target="tpu_custom_call" | custom-call | tf_op jit(solution)/shard_map/pallas_call | solution.py:491
  47.1 0.8 %copy.11 = bf16[64,2,8,128]{3,0,1,2:T(8,128)(2,1)} copy(bf16[64,2,8,128]{3,2,1,0:T(8,128)(2,1)S(1)} %bitcast.5) | data formatting | bytes 524288 | tf_op jit(solution)/shard_map/reshape | solution.py:549

commit v6 on v5

--- a/solution.py
+++ b/solution.py
@@ -385,20 +385,25 @@
     gather.finish()
 
     scale = s_all.shape[-1] ** (-0.5)
-    product = lax.dot_general(
-        held[...].reshape(512, 1024),
-        s_all[...],
-        (((1,), (1,)), ((), ())),
-        preferred_element_type=F32,
-    )
-    product = (product * scale).astype(BF16)
-    cells_f[0] = product[:, 0:128].astype(F32)
-    cells_f[1] = product[:, 128:256].astype(F32)
-    cells_out[...] = product[:, 128:256]
     copies = []
-    n = 4
-    copies.append(push(cells_out, cells_in, e_send.at[n], e_recv.at[n], sibling))
-    copies[0].start()
+    for m in range(2):
+        rows = slice(m * 256, m * 256 + 256)
+        product = lax.dot_general(
+            held[2 * m : 2 * m + 2].reshape(256, 1024),
+            s_all[...],
+            (((1,), (1,)), ((), ())),
+            preferred_element_type=F32,
+        )
+        product = (product * scale).astype(BF16)
+        cells_out[rows, :] = product[:, 128:256]
+        n = (4, 6)[m]
+        copy = push(
+            cells_out.at[rows], cells_in.at[rows], e_send.at[n], e_recv.at[n], sibling
+        )
+        copy.start()
+        copies.append(copy)
+        cells_f[0, rows, :] = product[:, 0:128].astype(F32)
+        cells_f[1, rows, :] = product[:, 128:256].astype(F32)
     for up, slots in enumerate(((0, 1), (6, 7))):
         for away in range(2):
             n = up * 2 + away
@@ -420,6 +425,7 @@
     patches = [(me // 6 + step) % 11 for step in range(11)]
     place(cells_f[0], core)
     copies[0].wait()
+    copies[1].wait()
     place(cells_in[...].astype(F32), 1 - core)
     for step, p in enumerate(patches):
         turned_part = x_t[pl.ds(pl.multiple_of(p * 96, 32), 128), :].T.astype(BF16)
@@ -430,7 +436,7 @@
     for c in range(5):
         target_chunk(c, every, x, xh, bias, w1, wh, w2, acc)
 
-    for copy in copies[1:]:
+    for copy in copies[2:]:
         copy.wait()
     for up, (inside, slots) in enumerate(((block < 3, (2, 3)), (block > 0, (0, 1)))):
         for away in range(2):
@@ -528,8 +534,8 @@
             pltpu.VMEM((9, 16, 128), F32),
             pltpu.SemaphoreType.DMA((38,)),
             pltpu.SemaphoreType.DMA((38,)),
-            pltpu.SemaphoreType.DMA((6,)),
-            pltpu.SemaphoreType.DMA((6,)),
+            pltpu.SemaphoreType.DMA((7,)),
+            pltpu.SemaphoreType.DMA((7,)),
             pltpu.SemaphoreType.DMA,
             pltpu.SemaphoreType.DMA,
         ],

time: 48 us -> 47.7 us (level)
  no operation moved by 1% of the time
where the time goes in v6:
time: 47.7 us; the launch traced here: 47.6 us
  Pallas kernels  46.8 us (98%)
  local copies, waits for them, and re-layouts  0.77 us (2%)
    pallas_call x1, Pallas kernels, on_device(): pl.pallas_call(whole_kernel, out_shape=pltpu.VMEM((64, 16, 128), BF16), i...  46.8 us

profile of v6, /device:TPU:1, one launch (start us, length us, event | category | flops | bytes accessed | tf_op | source)
XLA Modules:
  0.0 47.6 jit_solution(810931859275833833)
XLA Ops:
  0.0 46.8 %shard_map.82 = bf16[64,16,128]{2,1,0:T(8,128)(2,1)S(1)} custom-call(bf16[8,2,1024]{2,1,0:T(2,128)(2,1)} %t_given.1, bf16[128,1024]{1,0:T(8,128)(2,1)} %bitcast.6, f32[16,9]{1,0:T(8,128)} %t_in_given.1, f32[16]{0:T(128)} %t_bias_given.1, f32[16,9]{1,0:T(8,128)} %t_out_given.1, f32[16,9]{1,0:T(8,128)} %s_in_given.1, f32[16]{0:T(128)} %s_bias_given.1, ...), custom_call_target="tpu_custom_call" | custom-call | tf_op jit(solution)/shard_map/pallas_call | solution.py:497
  46.8 0.8 %copy.11 = bf16[64,2,8,128]{3,0,1,2:T(8,128)(2,1)} copy(bf16[64,2,8,128]{3,2,1,0:T(8,128)(2,1)S(1)} %bitcast.5) | data formatting | bytes 524288 | tf_op jit(solution)/shard_map/reshape | solution.py:555
